TPU v7x, 256 devices: a whole 4x4x8 slice. The times are simulated.
256 devices in a mesh: gx: 32 (over x, z), gy: 8 (over y, core).
Axes of the slice: x: 4, y: 4, z: 8, core: 2. Of those that a mesh axis runs over, the one named last changes fastest.
Arguments:
- fields: float32 [5, 3, 4096, 4096], P(None, None, 'gx', 'gy'), may hold values from -6 to 6
- metric_first: float32 [4096], P('gx'), may hold values from 0.5 to 2
- metric_second: float32 [4096], P('gy'), may hold values from 0.5 to 2
Outputs:
- slope_first: float32 [5, 3, 4096, 4096], P(None, None, 'gx', 'gy')
- slope_second: float32 [5, 3, 4096, 4096], P(None, None, 'gx', 'gy')
All inputs are finite; a program needn't handle non-finite values.
Results may differ from a plain program's by a relative error of at most 0.00007.
Values sent between devices are 32-bit elements; how exact they have to be, the bound alone decides.
No kernel may reach another device: no remote copies, remote signals or barrier semaphores. Data moves between devices by JAX's collectives and lax.ppermute only.
A program may use at most 128 MiB of HBM per device.

v0:
```python
import jax
import jax.numpy as jnp
from jax import lax
from jax.sharding import PartitionSpec as P

ALPHA = 0.47
COEF_A = 2.0 * (ALPHA + 2.0) / 3.0
COEF_B = (4.0 * ALPHA - 1.0) / 3.0
HIGHEST = lax.Precision.HIGHEST


def with_halo(cells, sides, width):
    for axis, dim in sides:
        count = lax.axis_size(axis)
        head = lax.slice_in_dim(cells, 0, width, axis=dim)
        tail = lax.slice_in_dim(cells, cells.shape[dim] - width, cells.shape[dim], axis=dim)
        cells = jnp.concatenate(
            [
                lax.ppermute(tail, axis, [(i, (i + 1) % count) for i in range(count)]),
                cells,
                lax.ppermute(head, axis, [((i + 1) % count, i) for i in range(count)]),
            ],
            axis=dim,
        )
    return cells


def from_behind(block, axis, distance):
    devices = range(lax.axis_size(axis))
    route = [((i - distance) % len(devices), i) for i in devices]
    return lax.ppermute(block, axis, route)


def explicit_side(padded, axis, extent):

    def shifted(offset):
        return lax.slice_in_dim(padded, 2 + offset, 2 + offset + extent, axis=axis)

    return COEF_A / 2.0 * (shifted(1) - shifted(-1)) + COEF_B / 4.0 * (shifted(2) - shifted(-2))


def line_inverse(extent):
    positions = jnp.arange(extent)
    diagonal = jnp.ones((extent,), jnp.float32)
    below_band = jnp.where(positions == 0, 0.0, ALPHA).astype(jnp.float32)
    above_band = jnp.where(positions == extent - 1, 0.0, ALPHA).astype(jnp.float32)
    return lax.linalg.tridiagonal_solve(
        below_band, diagonal, above_band, jnp.eye(extent, dtype=jnp.float32)
    )


def multiply_two(first_matrix, second_matrix):
    return jnp.matmul(first_matrix, second_matrix, precision=HIGHEST)


def invert_two(matrix):
    determinant = matrix[0, 0] * matrix[1, 1] - matrix[0, 1] * matrix[1, 0]
    adjugate = jnp.stack(
        [jnp.stack([matrix[1, 1], -matrix[0, 1]]), jnp.stack([-matrix[1, 0], matrix[0, 0]])]
    )
    return adjugate / determinant


def apply_two(matrix, values):
    return jnp.einsum("ij,j...->i...", matrix, values, precision=HIGHEST)


def reduced_blocks(inverse):
    zeroes = jnp.zeros((), jnp.float32)
    block_low = ALPHA * jnp.stack(
        [jnp.stack([zeroes, inverse[0, 0]]), jnp.stack([zeroes, inverse[-1, 0]])]
    )
    block_high = ALPHA * jnp.stack(
        [jnp.stack([inverse[0, -1], zeroes]), jnp.stack([inverse[-1, -1], zeroes])]
    )
    return (block_low, jnp.eye(2, dtype=jnp.float32), block_high)


def doubling(known, blocks, members, push):
    block_low, block_mid, block_high = blocks
    for section_number in range(members.bit_length() - 1):
        distance = 1 << section_number
        lower_term = push(known, distance)
        upper_term = push(known, -distance)
        inverse_mid = invert_two(block_mid)
        left_factor = multiply_two(block_low, inverse_mid)
        right_factor = multiply_two(block_high, inverse_mid)
        known = known - apply_two(left_factor, lower_term) - apply_two(right_factor, upper_term)
        block_mid = (
            block_mid
            - multiply_two(left_factor, block_high)
            - multiply_two(right_factor, block_low)
        )
        block_low = -multiply_two(left_factor, block_low)
        block_high = -multiply_two(right_factor, block_high)
    return apply_two(invert_two(block_low + block_mid + block_high), known)


def doubled(end_values, blocks, members, push):
    solved = doubling(end_values, blocks, members, push)
    return (push(solved[1], 1), push(solved[0], -1))


def piece_solve(force_first, force_second, reduce_first, reduce_second):
    inverse_first = line_inverse(force_first.shape[2])
    inverse_second = line_inverse(force_second.shape[3])
    local_first = jnp.einsum("ij,fpjk->fpik", inverse_first, force_first, precision=HIGHEST)
    local_second = jnp.einsum("fpkj,ij->fpki", force_second, inverse_second, precision=HIGHEST)
    ends_first = jnp.stack([local_first[:, :, 0, :], local_first[:, :, -1, :]])
    ends_second = jnp.stack([local_second[:, :, :, 0], local_second[:, :, :, -1]])
    left_value, right_value = reduce_first(ends_first, reduced_blocks(inverse_first))
    low_value, high_value = reduce_second(ends_second, reduced_blocks(inverse_second))
    compact_first = (
        local_first
        - ALPHA * left_value[:, :, None, :] * inverse_first[:, 0][:, None]
        - ALPHA * right_value[:, :, None, :] * inverse_first[:, -1][:, None]
    )
    compact_second = (
        local_second
        - ALPHA * low_value[..., None] * inverse_second[:, 0]
        - ALPHA * high_value[..., None] * inverse_second[:, -1]
    )
    return (compact_first, compact_second)


def shards(fields, metric_first, metric_second):
    extent_first = fields.shape[2]
    extent_second = fields.shape[3]
    width = 2
    padded = with_halo(fields, (("gx", 2), ("gy", 3)), width)
    force_first = explicit_side(padded[:, :, :, width:-width], 2, extent_first + 2 * width - 4)
    force_second = explicit_side(padded[:, :, width:-width, :], 3, extent_second + 2 * width - 4)
    compact_first, compact_second = piece_solve(
        force_first,
        force_second,
        lambda end_values, blocks: doubled(
            end_values,
            blocks,
            lax.axis_size("gx"),
            lambda values, distance: from_behind(values, "gx", distance),
        ),
        lambda end_values, blocks: doubled(
            end_values,
            blocks,
            lax.axis_size("gy"),
            lambda values, distance: from_behind(values, "gy", distance),
        ),
    )
    slope_first = metric_first[:, None] * compact_first
    slope_second = metric_second * compact_second
    return (slope_first, slope_second)


def solution(mesh):
    placed = (P(None, None, "gx", "gy"), P("gx"), P("gy"))
    return jax.shard_map(
        shards,
        mesh=mesh,
        in_specs=placed,
        out_specs=(P(None, None, "gx", "gy"), P(None, None, "gx", "gy")),
        check_vma=False,
    )
```

profile of v0, /device:TPU:1, one launch (start us, length us, event | category | flops | bytes accessed | tf_op | source)
XLA Modules:
  0.0 1977.1 jit_solution(4986502527108946891)
XLA Ops:
  14.2 976.1 %while.66 = (s32[]{:T(128)}, f32[]{:T(128)}, f32[512]{0:T(512)S(1)}, f32[15,32]{1,0:T(8,128)S(1)}, f32[15,32,512]{2,1,0:T(8,128)S(1)}, /*index=5*/f32[15,32]{1,0...) while((s32[]{:T(128)}, f32[]{:T(128)}, ...), condition=%wide.region_5.6_spmd, body=%wide.region_4.5_spmd.sunk | while | flops 49281 | bytes 534249 | solution.py:47
  57.2 20.0 %subtract_divide_fusion.125 = (f32[512]{0:T(512)S(1)}, f32[512]{0:T(512)S(1)}, f32[512]{0:T(512)S(1)}, f32[512]{0:T(512)S(1)}, f32[512]{0:T(512)S(1)}, /*index=5...) fusion(f32[512]{0:T(512)S(1)} %bitcast.3109, ...), kind=kLoop, calls=%fused_computation.264.clone.1 | loop fusion | flops 49152 | bytes 133376 | tf_op jit(solution)/shard_map/while/body/eval_jaxpr/div | solution.py:47
  122.3 20.0 %subtract_divide_fusion.125 = (f32[512]{0:T(512)S(1)}, f32[512]{0:T(512)S(1)}, f32[512]{0:T(512)S(1)}, f32[512]{0:T(512)S(1)}, f32[512]{0:T(512)S(1)}, /*index=5...) fusion(f32[512]{0:T(512)S(1)} %bitcast.3109, ...), kind=kLoop, calls=%fused_computation.264.clone.1 | loop fusion | flops 49152 | bytes 133376 | tf_op jit(solution)/shard_map/while/body/eval_jaxpr/div | solution.py:47
  187.4 20.0 %subtract_divide_fusion.125 = (f32[512]{0:T(512)S(1)}, f32[512]{0:T(512)S(1)}, f32[512]{0:T(512)S(1)}, f32[512]{0:T(512)S(1)}, f32[512]{0:T(512)S(1)}, /*index=5...) fusion(f32[512]{0:T(512)S(1)} %bitcast.3109, ...), kind=kLoop, calls=%fused_computation.264.clone.1 | loop fusion | flops 49152 | bytes 133376 | tf_op jit(solution)/shard_map/while/body/eval_jaxpr/div | solution.py:47
  252.4 20.0 %subtract_divide_fusion.125 = (f32[512]{0:T(512)S(1)}, f32[512]{0:T(512)S(1)}, f32[512]{0:T(512)S(1)}, f32[512]{0:T(512)S(1)}, f32[512]{0:T(512)S(1)}, /*index=5...) fusion(f32[512]{0:T(512)S(1)} %bitcast.3109, ...), kind=kLoop, calls=%fused_computation.264.clone.1 | loop fusion | flops 49152 | bytes 133376 | tf_op jit(solution)/shard_map/while/body/eval_jaxpr/div | solution.py:47
  317.5 20.0 %subtract_divide_fusion.125 = (f32[512]{0:T(512)S(1)}, f32[512]{0:T(512)S(1)}, f32[512]{0:T(512)S(1)}, f32[512]{0:T(512)S(1)}, f32[512]{0:T(512)S(1)}, /*index=5...) fusion(f32[512]{0:T(512)S(1)} %bitcast.3109, ...), kind=kLoop, calls=%fused_computation.264.clone.1 | loop fusion | flops 49152 | bytes 133376 | tf_op jit(solution)/shard_map/while/body/eval_jaxpr/div | solution.py:47
  382.6 20.0 %subtract_divide_fusion.125 = (f32[512]{0:T(512)S(1)}, f32[512]{0:T(512)S(1)}, f32[512]{0:T(512)S(1)}, f32[512]{0:T(512)S(1)}, f32[512]{0:T(512)S(1)}, /*index=5...) fusion(f32[512]{0:T(512)S(1)} %bitcast.3109, ...), kind=kLoop, calls=%fused_computation.264.clone.1 | loop fusion | flops 49152 | bytes 133376 | tf_op jit(solution)/shard_map/while/body/eval_jaxpr/div | solution.py:47
  447.7 20.0 %subtract_divide_fusion.125 = (f32[512]{0:T(512)S(1)}, f32[512]{0:T(512)S(1)}, f32[512]{0:T(512)S(1)}, f32[512]{0:T(512)S(1)}, f32[512]{0:T(512)S(1)}, /*index=5...) fusion(f32[512]{0:T(512)S(1)} %bitcast.3109, ...), kind=kLoop, calls=%fused_computation.264.clone.1 | loop fusion | flops 49152 | bytes 133376 | tf_op jit(solution)/shard_map/while/body/eval_jaxpr/div | solution.py:47
  512.7 20.0 %subtract_divide_fusion.125 = (f32[512]{0:T(512)S(1)}, f32[512]{0:T(512)S(1)}, f32[512]{0:T(512)S(1)}, f32[512]{0:T(512)S(1)}, f32[512]{0:T(512)S(1)}, /*index=5...) fusion(f32[512]{0:T(512)S(1)} %bitcast.3109, ...), kind=kLoop, calls=%fused_computation.264.clone.1 | loop fusion | flops 49152 | bytes 133376 | tf_op jit(solution)/shard_map/while/body/eval_jaxpr/div | solution.py:47
  577.8 20.0 %subtract_divide_fusion.125 = (f32[512]{0:T(512)S(1)}, f32[512]{0:T(512)S(1)}, f32[512]{0:T(512)S(1)}, f32[512]{0:T(512)S(1)}, f32[512]{0:T(512)S(1)}, /*index=5...) fusion(f32[512]{0:T(512)S(1)} %bitcast.3109, ...), kind=kLoop, calls=%fused_computation.264.clone.1 | loop fusion | flops 49152 | bytes 133376 | tf_op jit(solution)/shard_map/while/body/eval_jaxpr/div | solution.py:47
  642.9 20.0 %subtract_divide_fusion.125 = (f32[512]{0:T(512)S(1)}, f32[512]{0:T(512)S(1)}, f32[512]{0:T(512)S(1)}, f32[512]{0:T(512)S(1)}, f32[512]{0:T(512)S(1)}, /*index=5...) fusion(f32[512]{0:T(512)S(1)} %bitcast.3109, ...), kind=kLoop, calls=%fused_computation.264.clone.1 | loop fusion | flops 49152 | bytes 133376 | tf_op jit(solution)/shard_map/while/body/eval_jaxpr/div | solution.py:47
  707.9 20.0 %subtract_divide_fusion.125 = (f32[512]{0:T(512)S(1)}, f32[512]{0:T(512)S(1)}, f32[512]{0:T(512)S(1)}, f32[512]{0:T(512)S(1)}, f32[512]{0:T(512)S(1)}, /*index=5...) fusion(f32[512]{0:T(512)S(1)} %bitcast.3109, ...), kind=kLoop, calls=%fused_computation.264.clone.1 | loop fusion | flops 49152 | bytes 133376 | tf_op jit(solution)/shard_map/while/body/eval_jaxpr/div | solution.py:47
  773.0 20.0 %subtract_divide_fusion.125 = (f32[512]{0:T(512)S(1)}, f32[512]{0:T(512)S(1)}, f32[512]{0:T(512)S(1)}, f32[512]{0:T(512)S(1)}, f32[512]{0:T(512)S(1)}, /*index=5...) fusion(f32[512]{0:T(512)S(1)} %bitcast.3109, ...), kind=kLoop, calls=%fused_computation.264.clone.1 | loop fusion | flops 49152 | bytes 133376 | tf_op jit(solution)/shard_map/while/body/eval_jaxpr/div | solution.py:47
  838.1 20.0 %subtract_divide_fusion.125 = (f32[512]{0:T(512)S(1)}, f32[512]{0:T(512)S(1)}, f32[512]{0:T(512)S(1)}, f32[512]{0:T(512)S(1)}, f32[512]{0:T(512)S(1)}, /*index=5...) fusion(f32[512]{0:T(512)S(1)} %bitcast.3109, ...), kind=kLoop, calls=%fused_computation.264.clone.1 | loop fusion | flops 49152 | bytes 133376 | tf_op jit(solution)/shard_map/while/body/eval_jaxpr/div | solution.py:47
  903.2 20.0 %subtract_divide_fusion.125 = (f32[512]{0:T(512)S(1)}, f32[512]{0:T(512)S(1)}, f32[512]{0:T(512)S(1)}, f32[512]{0:T(512)S(1)}, f32[512]{0:T(512)S(1)}, /*index=5...) fusion(f32[512]{0:T(512)S(1)} %bitcast.3109, ...), kind=kLoop, calls=%fused_computation.264.clone.1 | loop fusion | flops 49152 | bytes 133376 | tf_op jit(solution)/shard_map/while/body/eval_jaxpr/div | solution.py:47
  968.2 20.0 %subtract_divide_fusion.125 = (f32[512]{0:T(512)S(1)}, f32[512]{0:T(512)S(1)}, f32[512]{0:T(512)S(1)}, f32[512]{0:T(512)S(1)}, f32[512]{0:T(512)S(1)}, /*index=5...) fusion(f32[512]{0:T(512)S(1)} %bitcast.3109, ...), kind=kLoop, calls=%fused_computation.264.clone.1 | loop fusion | flops 49152 | bytes 133376 | tf_op jit(solution)/shard_map/while/body/eval_jaxpr/div | solution.py:47
  1056.1 337.3 %while.67 = (s32[]{:T(128)}, f32[512]{0:T(512)S(1)}, f32[15,32,512]{2,1,0:T(8,128)S(1)}, f32[15,32,512]{2,1,0:T(8,128)S(1)}, f32[15,32]{1,0:T(8,128)}, /*index=5...) while((s32[]{:T(128)}, f32[512]{0:T(512)S(1)}, ...), condition=%wide.region_7.8_spmd, body=%wide.region_6.7_spmd.sunk | while | flops 32802 | bytes 531929 | solution.py:47
  1058.4 19.9 %multiply_subtract_fusion.125 = (f32[512]{0:T(512)S(1)}, f32[512]{0:T(512)S(1)}, f32[512]{0:T(512)S(1)}, f32[512]{0:T(512)S(1)}, f32[512]{0:T(512)S(1)}, /*index...) fusion(f32[512]{0:T(512)S(1)} %bitcast.3064, ...), kind=kLoop, calls=%fused_computation.330.clone.1 | loop fusion | flops 32768 | bytes 133248 | tf_op jit(solution)/shard_map/while/body/eval_jaxpr/sub | solution.py:47
  1080.9 19.9 %multiply_subtract_fusion.125 = (f32[512]{0:T(512)S(1)}, f32[512]{0:T(512)S(1)}, f32[512]{0:T(512)S(1)}, f32[512]{0:T(512)S(1)}, f32[512]{0:T(512)S(1)}, /*index...) fusion(f32[512]{0:T(512)S(1)} %bitcast.3064, ...), kind=kLoop, calls=%fused_computation.330.clone.1 | loop fusion | flops 32768 | bytes 133248 | tf_op jit(solution)/shard_map/while/body/eval_jaxpr/sub | solution.py:47
  1103.4 19.9 %multiply_subtract_fusion.125 = (f32[512]{0:T(512)S(1)}, f32[512]{0:T(512)S(1)}, f32[512]{0:T(512)S(1)}, f32[512]{0:T(512)S(1)}, f32[512]{0:T(512)S(1)}, /*index...) fusion(f32[512]{0:T(512)S(1)} %bitcast.3064, ...), kind=kLoop, calls=%fused_computation.330.clone.1 | loop fusion | flops 32768 | bytes 133248 | tf_op jit(solution)/shard_map/while/body/eval_jaxpr/sub | solution.py:47
  1125.9 19.9 %multiply_subtract_fusion.125 = (f32[512]{0:T(512)S(1)}, f32[512]{0:T(512)S(1)}, f32[512]{0:T(512)S(1)}, f32[512]{0:T(512)S(1)}, f32[512]{0:T(512)S(1)}, /*index...) fusion(f32[512]{0:T(512)S(1)} %bitcast.3064, ...), kind=kLoop, calls=%fused_computation.330.clone.1 | loop fusion | flops 32768 | bytes 133248 | tf_op jit(solution)/shard_map/while/body/eval_jaxpr/sub | solution.py:47
  1148.4 19.9 %multiply_subtract_fusion.125 = (f32[512]{0:T(512)S(1)}, f32[512]{0:T(512)S(1)}, f32[512]{0:T(512)S(1)}, f32[512]{0:T(512)S(1)}, f32[512]{0:T(512)S(1)}, /*index...) fusion(f32[512]{0:T(512)S(1)} %bitcast.3064, ...), kind=kLoop, calls=%fused_computation.330.clone.1 | loop fusion | flops 32768 | bytes 133248 | tf_op jit(solution)/shard_map/while/body/eval_jaxpr/sub | solution.py:47
  1170.8 19.9 %multiply_subtract_fusion.125 = (f32[512]{0:T(512)S(1)}, f32[512]{0:T(512)S(1)}, f32[512]{0:T(512)S(1)}, f32[512]{0:T(512)S(1)}, f32[512]{0:T(512)S(1)}, /*index...) fusion(f32[512]{0:T(512)S(1)} %bitcast.3064, ...), kind=kLoop, calls=%fused_computation.330.clone.1 | loop fusion | flops 32768 | bytes 133248 | tf_op jit(solution)/shard_map/while/body/eval_jaxpr/sub | solution.py:47
  1193.3 19.9 %multiply_subtract_fusion.125 = (f32[512]{0:T(512)S(1)}, f32[512]{0:T(512)S(1)}, f32[512]{0:T(512)S(1)}, f32[512]{0:T(512)S(1)}, f32[512]{0:T(512)S(1)}, /*index...) fusion(f32[512]{0:T(512)S(1)} %bitcast.3064, ...), kind=kLoop, calls=%fused_computation.330.clone.1 | loop fusion | flops 32768 | bytes 133248 | tf_op jit(solution)/shard_map/while/body/eval_jaxpr/sub | solution.py:47
  1215.8 19.9 %multiply_subtract_fusion.125 = (f32[512]{0:T(512)S(1)}, f32[512]{0:T(512)S(1)}, f32[512]{0:T(512)S(1)}, f32[512]{0:T(512)S(1)}, f32[512]{0:T(512)S(1)}, /*index...) fusion(f32[512]{0:T(512)S(1)} %bitcast.3064, ...), kind=kLoop, calls=%fused_computation.330.clone.1 | loop fusion | flops 32768 | bytes 133248 | tf_op jit(solution)/shard_map/while/body/eval_jaxpr/sub | solution.py:47
  1305.8 19.9 %multiply_subtract_fusion.125 = (f32[512]{0:T(512)S(1)}, f32[512]{0:T(512)S(1)}, f32[512]{0:T(512)S(1)}, f32[512]{0:T(512)S(1)}, f32[512]{0:T(512)S(1)}, /*index...) fusion(f32[512]{0:T(512)S(1)} %bitcast.3064, ...), kind=kLoop, calls=%fused_computation.330.clone.1 | loop fusion | flops 32768 | bytes 133248 | tf_op jit(solution)/shard_map/while/body/eval_jaxpr/sub | solution.py:47
  1328.2 19.9 %multiply_subtract_fusion.125 = (f32[512]{0:T(512)S(1)}, f32[512]{0:T(512)S(1)}, f32[512]{0:T(512)S(1)}, f32[512]{0:T(512)S(1)}, f32[512]{0:T(512)S(1)}, /*index...) fusion(f32[512]{0:T(512)S(1)} %bitcast.3064, ...), kind=kLoop, calls=%fused_computation.330.clone.1 | loop fusion | flops 32768 | bytes 133248 | tf_op jit(solution)/shard_map/while/body/eval_jaxpr/sub | solution.py:47
  1445.8 198.1 %while.64 = (s32[]{:T(128)}, f32[]{:T(128)}, f32[128]{0:T(128)S(1)}, f32[3,32]{1,0:T(4,128)S(1)}, f32[3,32,128]{2,1,0:T(8,128)S(1)}, /*index=5*/f32[3,32]{1,0:T(...) while((s32[]{:T(128)}, f32[]{:T(128)}, ...), condition=%wide.region_1.2_spmd, body=%wide.region_0.1_spmd.sunk | while | flops 12417 | bytes 103653 | solution.py:47
  1489.2 20.5 %fusion.655 = (f32[128]{0:T(128)S(1)}, f32[128]{0:T(128)S(1)}, f32[128]{0:T(128)S(1)}, f32[128]{0:T(128)S(1)}, f32[128]{0:T(128)S(1)}, /*index=5*/f32[128]{0:T(1...) fusion(f32[3,32,128]{2,1,0:T(8,128)S(1)} %get-tuple-element.222, ...), kind=kLoop, calls=%fused_computation.40.clone.1 | loop fusion | flops 12288 | bytes 33664 | tf_op jit(solution)/shard_map/while/body/eval_jaxpr/div | solution.py:47
  1555.3 20.5 %fusion.655 = (f32[128]{0:T(128)S(1)}, f32[128]{0:T(128)S(1)}, f32[128]{0:T(128)S(1)}, f32[128]{0:T(128)S(1)}, f32[128]{0:T(128)S(1)}, /*index=5*/f32[128]{0:T(1...) fusion(f32[3,32,128]{2,1,0:T(8,128)S(1)} %get-tuple-element.222, ...), kind=kLoop, calls=%fused_computation.40.clone.1 | loop fusion | flops 12288 | bytes 33664 | tf_op jit(solution)/shard_map/while/body/eval_jaxpr/div | solution.py:47
  1621.3 20.5 %fusion.655 = (f32[128]{0:T(128)S(1)}, f32[128]{0:T(128)S(1)}, f32[128]{0:T(128)S(1)}, f32[128]{0:T(128)S(1)}, f32[128]{0:T(128)S(1)}, /*index=5*/f32[128]{0:T(1...) fusion(f32[3,32,128]{2,1,0:T(8,128)S(1)} %get-tuple-element.222, ...), kind=kLoop, calls=%fused_computation.40.clone.1 | loop fusion | flops 12288 | bytes 33664 | tf_op jit(solution)/shard_map/while/body/eval_jaxpr/div | solution.py:47
  1703.9 64.2 %while.65 = (s32[]{:T(128)}, f32[128]{0:T(128)S(1)}, f32[3,32,128]{2,1,0:T(8,128)S(1)}, f32[3,32,128]{2,1,0:T(8,128)S(1)}, f32[3,32]{1,0:T(4,128)S(1)}, /*index=...) while((s32[]{:T(128)}, f32[128]{0:T(128)S(1)}, ...), condition=%wide.region_3.4_spmd, body=%wide.region_2.3_spmd.sunk | while | flops 8226 | bytes 101333 | solution.py:47
  (670 shorter events, 561.8 us)
Async XLA Ops:
  1.8 1852.5 %collective-permute-start.1 = (f32[5,3,2,512]{3,0,2,1:T(8,128)S(1)}, f32[5,3,2,512]{3,0,2,1:T(8,128)S(1)}, u32[]{:S(2)}, u32[]{:S(2)}) collective-permute-start(f32[5,3,2,512]{3,0,2,1:T(8,128)S(1)} %copy.88), channel_id=1, source_target_pairs={{0,8},{8,16},{16,24},{24,32},{32,40},{40,48},{48,56},{56,64},{64,7... | collective-permute-start | bytes 184328 | tf_op jit(solution)/shard_map/ppermute | solution.py:19
  4.3 1853.9 %collective-permute-start = (f32[5,3,2,512]{3,0,2,1:T(8,128)S(1)}, f32[5,3,2,512]{3,0,2,1:T(8,128)S(1)}, u32[]{:S(2)}, u32[]{:S(2)}) collective-permute-start(f32[5,3,2,512]{3,0,2,1:T(8,128)S(1)} %copy.87), channel_id=1, source_target_pairs={{8,0},{16,8},{24,16},{32,24},{40,32},{48,40},{56,48},{64,56},{72,6... | collective-permute-start | bytes 184328 | tf_op jit(solution)/shard_map/ppermute | solution.py:21
  1055.8 337.5 %copy-start.5 = (f32[1,512]{1,0:T(1,128)S(1)}, f32[1,512]{1,0:T(1,128)}, u32[]{:S(2)}) copy-start(f32[1,512]{1,0:T(1,128)} %get-tuple-element.940) | copy-start | bytes 6148
  1055.8 337.5 %copy-start.6 = (f32[1,512]{1,0:T(1,128)S(1)}, f32[1,512]{1,0:T(1,128)}, u32[]{:S(2)}) copy-start(f32[1,512]{1,0:T(1,128)} %get-tuple-element.941) | copy-start | bytes 6148
  1055.8 337.5 %copy-start.7 = (f32[1,512]{1,0:T(1,128)S(1)}, f32[1,512]{1,0:T(1,128)}, u32[]{:S(2)}) copy-start(f32[1,512]{1,0:T(1,128)} %get-tuple-element.942) | copy-start | bytes 6148
  1055.9 337.5 %copy-start.8 = (f32[1,512]{1,0:T(1,128)S(1)}, f32[1,512]{1,0:T(1,128)}, u32[]{:S(2)}) copy-start(f32[1,512]{1,0:T(1,128)} %get-tuple-element.943) | copy-start | bytes 6148
  1055.9 337.5 %copy-start.9 = (f32[1,512]{1,0:T(1,128)S(1)}, f32[1,512]{1,0:T(1,128)}, u32[]{:S(2)}) copy-start(f32[1,512]{1,0:T(1,128)} %get-tuple-element.944) | copy-start | bytes 6148
  1055.9 337.5 %copy-start.10 = (f32[1,512]{1,0:T(1,128)S(1)}, f32[1,512]{1,0:T(1,128)}, u32[]{:S(2)}) copy-start(f32[1,512]{1,0:T(1,128)} %get-tuple-element.945) | copy-start | bytes 6148
  1055.9 337.5 %copy-start.11 = (f32[1,512]{1,0:T(1,128)S(1)}, f32[1,512]{1,0:T(1,128)}, u32[]{:S(2)}) copy-start(f32[1,512]{1,0:T(1,128)} %get-tuple-element.946) | copy-start | bytes 6148
  1055.9 337.5 %copy-start.12 = (f32[1,512]{1,0:T(1,128)S(1)}, f32[1,512]{1,0:T(1,128)}, u32[]{:S(2)}) copy-start(f32[1,512]{1,0:T(1,128)} %get-tuple-element.947) | copy-start | bytes 6148
  1055.9 337.5 %copy-start.13 = (f32[1,512]{1,0:T(1,128)S(1)}, f32[1,512]{1,0:T(1,128)}, u32[]{:S(2)}) copy-start(f32[1,512]{1,0:T(1,128)} %get-tuple-element.948) | copy-start | bytes 6148
  1055.9 337.5 %copy-start.14 = (f32[1,512]{1,0:T(1,128)S(1)}, f32[1,512]{1,0:T(1,128)}, u32[]{:S(2)}) copy-start(f32[1,512]{1,0:T(1,128)} %get-tuple-element.949) | copy-start | bytes 6148
  1877.6 18.4 collective-permute-start.13
  1878.6 17.8 collective-permute-start.14
  1912.3 3.2 collective-permute-start.16
  1913.4 3.6 collective-permute-start.15
  1917.2 5.4 collective-permute-start.18
  1920.8 5.9 collective-permute-start.3
  1922.3 6.6 collective-permute-start.2
  1922.5 3.9 collective-permute-start.17
  1926.6 5.1 collective-permute-start.19
  1929.2 4.2 collective-permute-start.5
  1929.4 7.7 collective-permute-start.4
  1937.4 10.4 collective-permute-start.7
  1937.8 14.4 collective-permute-start.21
  1942.1 17.4 collective-permute-start.20
  1942.1 9.4 collective-permute-start.6
  1951.9 3.9 collective-permute-start.9
  1952.2 4.4 collective-permute-start.8
  1956.9 4.7 collective-permute-start.10
  1962.7 6.7 collective-permute-start.12
  1967.8 6.3 collective-permute-start.11
  (17 other events, 1130.0 us)
where the time goes:
time: 2020 us; the launch traced here: 1980 us
  other arithmetic  852 us (42%)
  loops' own time  742 us (37%)
  local copies, waits for them, and re-layouts  173 us (9%)
  between operations  113 us (6%)
  starting transfers between devices  40.2 us (2%)
  matrix products  32.8 us (2%)
  waiting for transfers between devices  24.4 us (1%)
    another operation x4, loops' own time, line_inverse(): lax.linalg.tridiagonal_solve(below_band, diagonal, above_band, jnp.eye(ex...  742 us
    div x20, other arithmetic, line_inverse(): lax.linalg.tridiagonal_solve(below_band, diagonal, above_band, jnp.eye(ex...  400 us
    sub x19, other arithmetic, line_inverse(): lax.linalg.tridiagonal_solve(below_band, diagonal, above_band, jnp.eye(ex...  378 us
    slice x194, local copies, waits for them, and re-layouts, line_inverse(): lax.linalg.tridiagonal_solve(below_band, diagonal, above_band, jnp.eye(ex...  93.4 us
    broadcast_in_dim x18, other arithmetic, line_inverse(): lax.linalg.tridiagonal_solve(below_band, diagonal, above_band, jnp.eye(ex...  41 us
  transfers between devices with their start and end apart: 22, of which 11 were waited for; matrix products, arithmetic and copies ran while one was open for 51% of the time, Pallas kernels for 0%

commit v1 on v0

v1 whole, which is shorter than its diff:
```python
import functools
import math
import numpy as np
import jax
import jax.numpy as jnp
from jax import lax
from jax.experimental import pallas as pl
from jax.experimental.pallas import tpu as pltpu
from jax.sharding import PartitionSpec as P

ALPHA = 0.47
STENCIL_NEAR = (ALPHA + 2.0) / 3.0
STENCIL_FAR = (4.0 * ALPHA - 1.0) / 12.0
ROOT = (math.sqrt(1.0 - 4.0 * ALPHA * ALPHA) - 1.0) / (2.0 * ALPHA)
PEAK = 1.0 / math.sqrt(1.0 - 4.0 * ALPHA * ALPHA)
DECAY = PEAK * (STENCIL_NEAR * (ROOT - 1.0 / ROOT) + STENCIL_FAR * (ROOT**2 - ROOT**-2))
NEXT = PEAK * STENCIL_FAR * (1.0 / ROOT - ROOT)
VMEM = 48 * 1024 * 1024


def kernel_matrix(extent):
    gap = np.arange(extent)[:, None] - np.arange(extent)[None, :]
    size = np.abs(gap)
    value = DECAY * ROOT ** size.astype(np.float64) + NEXT * (size == 1)
    return np.sign(gap) * value


def border_columns(extent):
    place = np.arange(extent)
    left = DECAY * ROOT ** place.astype(np.float64)
    return np.stack([left, -left[::-1], NEXT * (place == 0), -NEXT * (place == extent - 1)])


def split(value):
    high = value.astype(jnp.bfloat16)
    return high, (value - high.astype(jnp.float32)).astype(jnp.bfloat16)


def dot(left, right):
    return jnp.dot(left, right, preferred_element_type=jnp.float32)


def stacked(rows):
    high = rows.astype(jnp.bfloat16).astype(jnp.float32)
    low = (rows - high).astype(jnp.bfloat16).astype(jnp.float32)
    return jnp.concatenate([high, low, high, jnp.zeros_like(high)], axis=0).astype(jnp.bfloat16)


def moments_kernel(step, place_ref, u_ref, wx_ref, wy_ref, mx_ref, ox_ref, my_ref, oy_ref):
    g = pl.program_id(0)
    px = place_ref[0]
    py = place_ref[1]
    extent, width = u_ref.shape[1:]
    for t in range(step):
        f = g * step + t
        u = u_ref[t]
        right = jnp.zeros((8, width), jnp.float32)
        left = jnp.zeros((8, width), jnp.float32)
        for i in range(0, extent, 8):
            rows = u_ref[t, i : i + 8]
            right = right + rows * wx_ref[0, i : i + 8]
            left = left + rows * wx_ref[1, i : i + 8]
        mx_ref[0, pl.ds(f, 1), :] = jnp.sum(right, axis=0, keepdims=True)
        mx_ref[1, pl.ds(f, 1), :] = jnp.sum(left, axis=0, keepdims=True)
        head = u_ref[t, 0:1]
        tail = u_ref[t, extent - 1 : extent]
        mx_ref[2, pl.ds(f, 1), :] = jnp.where(px == 0, tail, head)
        ox_ref[pl.ds(f, 1), :] = jnp.where(px == 0, head, tail)
        half = width // 2
        turned = [u[:, c : c + 128].T for c in range(0, width, 128)]
        sums = []
        for side in range(2):
            for part in range(2):
                total = jnp.zeros((8, extent), jnp.float32)
                for j in range(part * half, (part + 1) * half, 8):
                    total = total + turned[j // 128][j % 128 : j % 128 + 8] * wy_ref[side, j - part * half : j - part * half + 8]
                sums.append(jnp.sum(total, axis=0, keepdims=True))
        low, high = turned[0][0:1], turned[-1][127:128]
        whole = ROOT**half
        my_ref[0, pl.ds(f, 1), :] = sums[1] + whole * sums[0]
        my_ref[1, pl.ds(f, 1), :] = sums[2] + whole * sums[3]
        my_ref[2, pl.ds(f, 1), :] = jnp.where(py == 0, high, low)
        oy_ref[0, pl.ds(f, 1), :] = jnp.where(py == 0, low, high)
        oy_ref[1, pl.ds(f, 1), :] = sums[0]
        oy_ref[2, pl.ds(f, 1), :] = sums[3]
        oy_ref[3, pl.ds(f, 1), :] = turned[half // 128 - 1][127:128]
        oy_ref[4, pl.ds(f, 1), :] = turned[half // 128][0:1]


def moments(place, cells, step=5):
    count, extent, width = cells.shape
    power = ROOT ** np.arange(1, extent + 1, dtype=np.float64)
    wx = np.broadcast_to(np.stack([power[::-1], power])[:, :, None], (2, extent, width)).astype(np.float32)
    power = ROOT ** np.arange(1, width // 2 + 1, dtype=np.float64)
    wy = np.broadcast_to(np.stack([power[::-1], power])[:, :, None], (2, width // 2, extent)).astype(np.float32)
    whole = lambda *shape: pl.BlockSpec(shape, lambda g: (0,) * len(shape))
    out = lambda *shape: jax.ShapeDtypeStruct(shape, jnp.float32)
    return pl.pallas_call(
        functools.partial(moments_kernel, step),
        grid=(count // step,),
        in_specs=[
            pl.BlockSpec(memory_space=pltpu.SMEM),
            pl.BlockSpec((step, extent, width), lambda g: (g, 0, 0)),
            whole(2, extent, width),
            whole(2, width // 2, extent),
        ],
        out_specs=[whole(3, count, width), whole(count, width), whole(3, count, extent), whole(5, count, extent)],
        out_shape=[out(3, count, width), out(count, width), out(3, count, extent), out(5, count, extent)],
        compiler_params=pltpu.CompilerParams(vmem_limit_bytes=VMEM),
        name="moments",
    )(place, cells, jnp.asarray(wx), jnp.asarray(wy))


def first_kernel(step, u_ref, v_ref, metric_ref, h_ref, c_ref, out_ref, one_ref, two_ref):
    g = pl.program_id(0)
    extent = u_ref.shape[1]

    @pl.when(g == 0)
    def _():
        row = lax.broadcasted_iota(jnp.int32, (extent, extent), 0)
        column = lax.broadcasted_iota(jnp.int32, (extent, extent), 1)
        metric = jnp.sum(jnp.where(row == column, metric_ref[...], 0.0), axis=1, keepdims=True)
        high, low = split(h_ref[...] * metric)
        one_ref[:, :extent] = high
        one_ref[:, extent:] = high
        two_ref[:, :extent] = low
        scaled = c_ref[...] * metric
        c_high = scaled.astype(jnp.bfloat16)
        c_low = (scaled - c_high.astype(jnp.float32)).astype(jnp.bfloat16)
        lane = lax.broadcasted_iota(jnp.int32, scaled.shape, 1)
        two_ref[:, extent:] = jnp.where(lane < 16, c_high.astype(jnp.float32), c_low.astype(jnp.float32)).astype(jnp.bfloat16)

    for t in range(step):
        f = g * step + t
        high, low = split(u_ref[t])
        rows = jnp.concatenate([v_ref[k, pl.ds(f, 1), :] for k in range(4)] + [jnp.zeros((4, u_ref.shape[2]), jnp.float32)], axis=0)
        total = dot(one_ref[...], jnp.concatenate([high, low], axis=0))
        total = total + dot(two_ref[...], jnp.concatenate([high, stacked(rows)], axis=0))
        out_ref[t] = total


def first(cells, border, metric, step=5):
    count, extent, width = cells.shape
    h = kernel_matrix(extent).astype(np.float32)
    c = np.zeros((extent, 32), np.float64)
    columns = border_columns(extent)
    for k in range(3):
        c[:, 8 * k : 8 * k + 4] = columns.T
    whole = lambda *shape: pl.BlockSpec(shape, lambda g: (0,) * len(shape))
    return pl.pallas_call(
        functools.partial(first_kernel, step),
        grid=(count // step,),
        in_specs=[
            pl.BlockSpec((step, extent, width), lambda g: (g, 0, 0)),
            whole(4, count, width),
            whole(1, extent),
            whole(extent, extent),
            whole(extent, 32),
        ],
        out_specs=pl.BlockSpec((step, extent, width), lambda g: (g, 0, 0)),
        out_shape=jax.ShapeDtypeStruct(cells.shape, jnp.float32),
        scratch_shapes=[pltpu.VMEM((extent, 2 * extent), jnp.bfloat16), pltpu.VMEM((extent, extent + 32), jnp.bfloat16)],
        compiler_params=pltpu.CompilerParams(vmem_limit_bytes=VMEM),
        name="slope_first",
    )(cells, border, metric.reshape(1, extent), jnp.asarray(h), jnp.asarray(c.astype(np.float32)))


def second_kernel(step, u_ref, v_ref, metric_ref, h_ref, c_ref, out_ref):
    g = pl.program_id(0)
    extent, width = u_ref.shape[1:]
    half = width // 2
    metric = metric_ref[...]
    for t in range(step):
        f = g * step + t
        rows = stacked(jnp.concatenate([v_ref[k, pl.ds(f, 1), :] for k in range(8)], axis=0))
        for part in range(2):
            at = slice(part * half, (part + 1) * half)
            high, low = split(u_ref[t, :, at])
            total = dot(high, h_ref[0]) + dot(low, h_ref[0]) + dot(high, h_ref[1])
            total = total + lax.dot_general(rows, c_ref[:, at], (((0,), (0,)), ((), ())), preferred_element_type=jnp.float32)
            out_ref[t, :, at] = total * metric[:, at]


def second(cells, border, metric, step=5):
    count, extent, width = cells.shape
    half = width // 2
    def halves(value):
        high = value.astype(np.float32).astype(jnp.bfloat16)
        return high, (value - high.astype(np.float64)).astype(np.float32).astype(jnp.bfloat16)
    h = np.stack(halves(kernel_matrix(half).T))
    c = np.zeros((8, width), np.float64)
    c[:4, :half] = border_columns(half)
    c[4:, half:] = border_columns(half)
    high, low = halves(c)
    c = np.concatenate([high, high, low, np.zeros_like(high)])
    whole = lambda *shape: pl.BlockSpec(shape, lambda g: (0,) * len(shape))
    return pl.pallas_call(
        functools.partial(second_kernel, step),
        grid=(count // step,),
        in_specs=[
            pl.BlockSpec((step, extent, width), lambda g: (g, 0, 0)),
            whole(8, count, extent),
            whole(1, width),
            whole(2, half, half),
            whole(32, width),
        ],
        out_specs=pl.BlockSpec((step, extent, width), lambda g: (g, 0, 0)),
        out_shape=jax.ShapeDtypeStruct(cells.shape, jnp.float32),
        compiler_params=pltpu.CompilerParams(vmem_limit_bytes=VMEM),
        name="slope_second",
    )(cells, border, metric.reshape(1, width), jnp.asarray(h), jnp.asarray(c))


def scan_table(devices, extent):
    levels = devices.bit_length() - 1
    table = np.zeros((devices, 6 * levels + 2), np.float64)
    ratio = ROOT**extent
    for d in range(devices):
        for k in range(levels):
            size = 1 << k
            weight = ratio**size
            upper = d >> k & 1
            place = d % size
            table[d, 6 * k : 6 * k + 6] = (
                (1.0, weight, weight, 1.0, ratio**place, 0.0)
                if upper
                else (weight, 1.0, 1.0, weight, 0.0, ratio ** (size - 1 - place))
            )
        table[d, -2:] = np.array([ratio**d, ratio ** (devices - 1 - d)]) / (1.0 - ratio**devices)
    return table.astype(np.float32)


def swap(block, axis, mask):
    return lax.ppermute(block, axis, [(i, i ^ mask) for i in range(lax.axis_size(axis))])


def swap_odd(block, axis):
    count = lax.axis_size(axis)
    return lax.ppermute(block, axis, [(i, (i + (1 if i % 2 else -1)) % count) for i in range(count)])


def gathered(message, spare, axis, extent, masks):
    count = lax.axis_size(axis)
    index = lax.axis_index(axis)
    row = lax.dynamic_index_in_dim(jnp.asarray(scan_table(count, extent)), index, keepdims=False)
    pair = lambda k: row[k : k + 2][:, None, None]
    other_edge = swap_odd(spare, axis)
    total = message[:2]
    outside = None
    for k, mask in enumerate(masks):
        reply = swap(message if k == 0 else total, axis, mask)
        if k == 0:
            edge = reply[2]
        term = pair(6 * k + 4) * reply[:2]
        outside = term if outside is None else outside + term
        total = pair(6 * k) * total + pair(6 * k + 2) * reply[:2]
    outside = outside + pair(6 * len(masks)) * total
    even = index % 2 == 0
    edges = jnp.stack([jnp.where(even, other_edge, edge), jnp.where(even, edge, other_edge)])
    return outside, edges


def shards(fields, metric_first, metric_second):
    fields_count, planes, extent, width = fields.shape
    cells = fields.reshape(fields_count * planes, extent, width)
    place = jnp.stack([lax.axis_index("gx") % 2, lax.axis_index("gy") % 2]).astype(jnp.int32)
    message_x, spare_x, message_y, own_y = moments(place, cells)
    outside_y, edges_y = gathered(message_y, own_y[0], "gy", width, (1, 2, 6))
    outside_x, edges_x = gathered(message_x, spare_x, "gx", extent, (1, 2, 7, 8, 24))
    ratio = ROOT ** (width // 2)
    border_y = jnp.stack(
        [
            outside_y[0],
            own_y[2] + ratio * outside_y[1],
            edges_y[0],
            own_y[4],
            own_y[1] + ratio * outside_y[0],
            outside_y[1],
            own_y[3],
            edges_y[1],
        ]
    )
    slope_second = second(cells, border_y, metric_second)
    slope_first = first(cells, jnp.concatenate([outside_x, edges_x]), metric_first)
    return slope_first.reshape(fields.shape), slope_second.reshape(fields.shape)


def solution(mesh):
    return jax.shard_map(
        shards,
        mesh=mesh,
        in_specs=(P(None, None, "gx", "gy"), P("gx"), P("gy")),
        out_specs=(P(None, None, "gx", "gy"), P(None, None, "gx", "gy")),
        check_vma=False,
    )
```

time: 2020 us -> 55.9 us (0.03)
  the two profiles are of different devices: /device:TPU:1 before, /device:TPU:32 now
where the time goes in v1:
time: 55.9 us; the launch traced here: 55.7 us
  waiting for transfers between devices  23.2 us (42%)
  starting transfers between devices  13.8 us (25%)
  Pallas kernels  9.21 us (16%)
  local copies, waits for them, and re-layouts  7.8 us (14%)
  between operations  0.86 us (2%)
  other arithmetic  0.76 us (1%)
    ppermute x8, waiting for transfers between devices, swap(): lax.ppermute(block, axis, [(i, i ^ mask) for i in range(lax.axis_size(axi...  19 us
    ppermute x8, starting transfers between devices, swap(): lax.ppermute(block, axis, [(i, i ^ mask) for i in range(lax.axis_size(axi...  11.8 us
    unnamed x24, local copies, waits for them, and re-layouts  6.25 us
    ppermute x2, waiting for transfers between devices, swap_odd(): lax.ppermute(block, axis, [(i, (i + (1 if i % 2 else -1)) % count) for i...  4.19 us
    pallas_call x1, Pallas kernels, second(): pl.pallas_call(functools.partial(second_kernel, step), grid=(count // ste...  3.82 us
    pallas_call x1, Pallas kernels, first(): pl.pallas_call(functools.partial(first_kernel, step), grid=(count // step...  3.32 us
    pallas_call x1, Pallas kernels, moments(): pl.pallas_call(functools.partial(moments_kernel, step), grid=(count // st...  2.07 us
    ppermute x2, starting transfers between devices, swap_odd(): lax.ppermute(block, axis, [(i, (i + (1 if i % 2 else -1)) % count) for i...  2.01 us
  transfers between devices with their start and end apart: 10, of which 6 were waited for; matrix products, arithmetic and copies ran while one was open for 4% of the time, Pallas kernels for 7%

profile of v1, /device:TPU:32, one launch (start us, length us, event | category | flops | bytes accessed | tf_op | source)
XLA Modules:
  0.0 55.7 jit_solution(17354212715708721470)
XLA Ops:
  0.8 2.1 %copy-done = f32[5,3,128,512]{3,2,1,0:T(8,128)S(1)} copy-done((f32[5,3,128,512]{3,2,1,0:T(8,128)S(1)}, f32[5,3,128,512]{3,2,1,0:T(8,128)}, u32[]{:S(2)}) %copy-start) | copy-done | bytes 3932184
  2.9 1.0 %copy-done.2 = f32[2,128,512]{2,1,0:T(8,128)S(1)} copy-done((f32[2,128,512]{2,1,0:T(8,128)S(1)}, f32[2,128,512]{2,1,0:T(8,128)}, u32[]{:S(2)}) %copy-start.2) | copy-done | bytes 524312
  3.9 0.9 %copy-done.4 = f32[2,256,128]{2,1,0:T(8,128)S(1)} copy-done((f32[2,256,128]{2,1,0:T(8,128)S(1)}, f32[2,256,128]{2,1,0:T(8,128)}, u32[]{:S(2)}) %copy-start.4) | copy-done | bytes 262168
  4.9 2.1 %moments.1 = (f32[3,15,512]{2,1,0:T(8,128)S(1)}, f32[15,512]{1,0:T(8,128)S(1)}, f32[3,15,128]{2,1,0:T(8,128)S(1)}, f32[5,15,128]{2,1,0:T(8,128)S(1)}) custom-call(s32[2]{0:T(128)S(1)} %pad_add_fusion.place_ref, f32[15,128,512]{2,1,0:T(8,128)S(1)} %bitcast.81, f32[2,128,512]{2,1,0:T(8,128)S(1)} %copy-done.2, f32[2,256,128]{2,1,0:T(8,128)S(1)} %copy-done.4), custom_call_target="tpu_custom_call" | custom-call | tf_op jit(solution)/shard_map/moments/pallas_call | solution.py:98
  6.9 0.1 collective-permute-start.6
  7.0 0.7 %constant_dynamic-slice_fusion = f32[1,20]{1,0:T(1,128)S(1)} fusion(f32[8,20]{1,0:T(8,128)} %constant.61.clone, s32[]{:T(128)S(6)} %select_n.53), kind=kLoop, calls=%fused_computation.49 | loop fusion | bytes 164 | tf_op jit(solution)/shard_map/jit(dynamic_index_in_dim)/dynamic_slice | solution.py:245
  7.7 0.1 slice_bitcast_fusion.12
  7.8 0.4 collective-permute-done.6
  8.3 1.6 %collective-permute-start.7 = (f32[2,15,128]{2,1,0:T(8,128)S(1)}, f32[2,15,128]{2,1,0:T(8,128)S(1)}, u32[]{:S(2)}, u32[]{:S(2)}) collective-permute-start(f32[2,15,128]{2,1,0:T(8,128)S(1)} %multiply_add_fusion.7), channel_id=1, source_target_pairs={{0,2},{1,3},{2,0},{3,1},{4,6},{5,7},{6,4},{7,5},{8,10},{9,11},{10,... | collective-permute-start | bytes 46088 | tf_op jit(solution)/shard_map/ppermute | solution.py:234
  9.9 1.9 %collective-permute-start.5 = (f32[15,512]{1,0:T(8,128)S(1)}, f32[15,512]{1,0:T(8,128)S(1)}, u32[]{:S(2)}, u32[]{:S(2)}) collective-permute-start(f32[15,512]{1,0:T(8,128)S(1)} %get-tuple-element.7), channel_id=1, source_target_pairs={{0,248},{8,16},{16,8},{24,32},{32,24},{40,48},{48,40},{56,64},{64,... | collective-permute-start | bytes 92168 | tf_op jit(solution)/shard_map/ppermute | solution.py:239
  11.8 6.2 %collective-permute-start = (f32[3,15,512]{2,1,0:T(8,128)S(1)}, f32[3,15,512]{2,1,0:T(8,128)S(1)}, u32[]{:S(2)}, u32[]{:S(2)}) collective-permute-start(f32[3,15,512]{2,1,0:T(8,128)S(1)} %get-tuple-element.6), channel_id=1, source_target_pairs={{0,8},{8,0},{16,24},{24,16},{32,40},{40,32},{48,56},{56,48},{64,72... | collective-permute-start | bytes 276488 | tf_op jit(solution)/shard_map/ppermute | solution.py:234
  18.1 2.2 %collective-permute-start.8 = (f32[2,15,128]{2,1,0:T(8,128)S(1)}, f32[2,15,128]{2,1,0:T(8,128)S(1)}, u32[]{:S(2)}, u32[]{:S(2)}) collective-permute-start(f32[2,15,128]{2,1,0:T(8,128)S(1)} %multiply_add_fusion.6), channel_id=1, source_target_pairs={{0,6},{1,7},{2,4},{3,5},{4,2},{5,3},{6,0},{7,1},{8,14},{9,15},{10,... | collective-permute-start | bytes 46088 | tf_op jit(solution)/shard_map/ppermute | solution.py:234
  20.3 0.7 %constant_dynamic-slice_fusion.1 = f32[1,32]{1,0:T(1,128)S(1)} fusion(f32[32,32]{1,0:T(8,128)} %constant.62.clone, s32[]{:T(128)S(6)} %select_n.47), kind=kLoop, calls=%fused_computation.50 | loop fusion | bytes 260 | tf_op jit(solution)/shard_map/jit(dynamic_index_in_dim)/dynamic_slice | solution.py:245
  21.0 2.1 %collective-permute-done.8 = f32[2,15,128]{2,1,0:T(8,128)S(1)} collective-permute-done((f32[2,15,128]{2,1,0:T(8,128)S(1)}, f32[2,15,128]{2,1,0:T(8,128)S(1)}, u32[]{:S(2)}, u32[]{:S(2)}) %collective-permute-start.8) | collective-permute-done | bytes 15392 | tf_op jit(solution)/shard_map/ppermute | solution.py:234
  23.1 0.1 multiply_add_fusion.5
  23.2 0.1 collective-permute-start.9
  23.3 0.1 slice_bitcast_fusion.28
  23.4 4.2 %collective-permute-done.9 = f32[15,128]{1,0:T(8,128)S(1)} collective-permute-done((f32[15,128]{1,0:T(8,128)S(1)}, f32[15,128]{1,0:T(8,128)S(1)}, u32[]{:S(2)}, u32[]{:S(2)}) %collective-permute-start.9) | collective-permute-done | bytes 7712 | tf_op jit(solution)/shard_map/ppermute | solution.py:239
  27.6 0.1 multiply_add_fusion.4
  27.7 0.1 collective-permute-start.1
  27.8 5.1 %collective-permute-done.1 = f32[2,15,512]{2,1,0:T(8,128)S(1)} collective-permute-done((f32[2,15,512]{2,1,0:T(8,128)S(1)}, f32[2,15,512]{2,1,0:T(8,128)S(1)}, u32[]{:S(2)}, u32[]{:S(2)}) %collective-permute-start.1) | collective-permute-done | bytes 61472 | tf_op jit(solution)/shard_map/ppermute | solution.py:234
  32.9 0.1 multiply_add_fusion.3
  33.0 0.1 collective-permute-start.2
  33.1 7.2 %collective-permute-done.2 = f32[2,15,512]{2,1,0:T(8,128)S(1)} collective-permute-done((f32[2,15,512]{2,1,0:T(8,128)S(1)}, f32[2,15,512]{2,1,0:T(8,128)S(1)}, u32[]{:S(2)}, u32[]{:S(2)}) %collective-permute-start.2) | collective-permute-done | bytes 61472 | tf_op jit(solution)/shard_map/ppermute | solution.py:234
  40.4 0.1 collective-permute-start.3
  40.6 2.1 %copy-done.1 = f32[5,3,128,512]{3,2,1,0:T(8,128)S(1)} copy-done((f32[5,3,128,512]{3,2,1,0:T(8,128)S(1)}, f32[5,3,128,512]{3,2,1,0:T(8,128)}, u32[]{:S(2)}) %copy-start.1) | copy-done | bytes 3932184
  42.7 3.8 %slope_second.1 = f32[15,128,512]{2,1,0:T(8,128)} custom-call(f32[15,128,512]{2,1,0:T(8,128)S(1)} %bitcast.82, f32[8,15,128]{2,1,0:T(8,128)S(1)} %constant_dynamic-update-slice_fusion.v_ref, f32[1,512]{1,0:T(1,128)S(1)} %bitcast.84, bf16[2,256,256]{2,1,0:T(8,128)(2,1)S(1)} %copy-done.3, bf16[32,512]{1,0:T(8,128)(2,1)S(1)} %copy-done.7), custom_call_target="tpu_custom_call" | custom-call | tf_op jit(solution)/shard_map/slope_second/pallas_call | solution.py:197
  46.5 0.1 multiply_add_fusion.1
  46.6 1.4 %collective-permute-start.4 = (f32[2,15,512]{2,1,0:T(8,128)S(1)}, f32[2,15,512]{2,1,0:T(8,128)S(1)}, u32[]{:S(2)}, u32[]{:S(2)}) collective-permute-start(f32[2,15,512]{2,1,0:T(8,128)S(1)} %multiply_add_fusion.1), channel_id=1, source_target_pairs={{0,192},{8,200},{16,208},{24,216},{32,224},{40,232},{48,240},{56,2... | collective-permute-start | bytes 184328 | tf_op jit(solution)/shard_map/ppermute | solution.py:234
  48.0 4.1 %collective-permute-done.4 = f32[2,15,512]{2,1,0:T(8,128)S(1)} collective-permute-done((f32[2,15,512]{2,1,0:T(8,128)S(1)}, f32[2,15,512]{2,1,0:T(8,128)S(1)}, u32[]{:S(2)}, u32[]{:S(2)}) %collective-permute-start.4) | collective-permute-done | bytes 61472 | tf_op jit(solution)/shard_map/ppermute | solution.py:234
  52.2 0.1 multiply_add_fusion
  52.3 3.3 %slope_first.1 = f32[15,128,512]{2,1,0:T(8,128)} custom-call(f32[15,128,512]{2,1,0:T(8,128)S(1)} %bitcast.83, f32[4,15,512]{2,1,0:T(8,128)S(1)} %pad_maximum_fusion.v_ref, f32[1,128]{1,0:T(1,128)S(1)} %bitcast.85, f32[128,128]{1,0:T(8,128)S(1)} %copy-done.6, f32[128,32]{1,0:T(8,128)S(1)} %copy-done.5), custom_call_target="tpu_custom_call" | custom-call | tf_op jit(solution)/shard_map/slope_first/pallas_call | solution.py:150
  (34 shorter events, 0.4 us)
Async XLA Ops:
  0.6 39.9 %copy-start.7 = (bf16[32,512]{1,0:T(8,128)(2,1)S(1)}, bf16[32,512]{1,0:T(8,128)(2,1)}, u32[]{:S(2)}) copy-start(bf16[32,512]{1,0:T(8,128)(2,1)} %constant.64.clone.c_ref) | copy-start | bytes 98308
  0.6 39.9 %copy-start.8 = (f32[512]{0:T(512)S(1)}, f32[512]{0:T(512)}, u32[]{:S(2)}) copy-start(f32[512]{0:T(512)} %param.13) | copy-start | bytes 6148
  0.7 2.1 %copy-start = (f32[5,3,128,512]{3,2,1,0:T(8,128)S(1)}, f32[5,3,128,512]{3,2,1,0:T(8,128)}, u32[]{:S(2)}) copy-start(f32[5,3,128,512]{3,2,1,0:T(8,128)} %param.11) | copy-start | bytes 11796484
  2.9 1.0 %copy-start.2 = (f32[2,128,512]{2,1,0:T(8,128)S(1)}, f32[2,128,512]{2,1,0:T(8,128)}, u32[]{:S(2)}) copy-start(f32[2,128,512]{2,1,0:T(8,128)} %constant.59.clone.wx_ref) | copy-start | bytes 1572868
  3.9 0.9 %copy-start.4 = (f32[2,256,128]{2,1,0:T(8,128)S(1)}, f32[2,256,128]{2,1,0:T(8,128)}, u32[]{:S(2)}) copy-start(f32[2,256,128]{2,1,0:T(8,128)} %constant.60.clone.wy_ref) | copy-start | bytes 786436
  4.9 35.7 %copy-start.3 = (bf16[2,256,256]{2,1,0:T(8,128)(2,1)S(1)}, bf16[2,256,256]{2,1,0:T(8,128)(2,1)}, u32[]{:S(2)}) copy-start(bf16[2,256,256]{2,1,0:T(8,128)(2,1)} %constant.63.clone.h_ref) | copy-start | bytes 786436
  6.9 1.3 %collective-permute-start.6 = (f32[3,15,128]{2,1,0:T(8,128)S(1)}, f32[3,15,128]{2,1,0:T(8,128)S(1)}, u32[]{:S(2)}, u32[]{:S(2)}) collective-permute-start(f32[3,15,128]{2,1,0:T(8,128)S(1)} %get-tuple-element.8), channel_id=1, source_target_pairs={{0,1},{1,0},{2,3},{3,2},{4,5},{5,4},{6,7},{7,6},{8,9},{9,8},{10,11... | collective-permute-start | bytes 69128 | tf_op jit(solution)/shard_map/ppermute | solution.py:234
  8.3 9.8 %collective-permute-start.7 = (f32[2,15,128]{2,1,0:T(8,128)S(1)}, f32[2,15,128]{2,1,0:T(8,128)S(1)}, u32[]{:S(2)}, u32[]{:S(2)}) collective-permute-start(f32[2,15,128]{2,1,0:T(8,128)S(1)} %multiply_add_fusion.7), channel_id=1, source_target_pairs={{0,2},{1,3},{2,0},{3,1},{4,6},{5,7},{6,4},{7,5},{8,10},{9,11},{10,... | collective-permute-start | bytes 46088 | tf_op jit(solution)/shard_map/ppermute | solution.py:234
  9.9 38.1 %collective-permute-start.5 = (f32[15,512]{1,0:T(8,128)S(1)}, f32[15,512]{1,0:T(8,128)S(1)}, u32[]{:S(2)}, u32[]{:S(2)}) collective-permute-start(f32[15,512]{1,0:T(8,128)S(1)} %get-tuple-element.7), channel_id=1, source_target_pairs={{0,248},{8,16},{16,8},{24,32},{32,24},{40,48},{48,40},{56,64},{64,... | collective-permute-start | bytes 92168 | tf_op jit(solution)/shard_map/ppermute | solution.py:239
  11.8 15.8 %collective-permute-start = (f32[3,15,512]{2,1,0:T(8,128)S(1)}, f32[3,15,512]{2,1,0:T(8,128)S(1)}, u32[]{:S(2)}, u32[]{:S(2)}) collective-permute-start(f32[3,15,512]{2,1,0:T(8,128)S(1)} %get-tuple-element.6), channel_id=1, source_target_pairs={{0,8},{8,0},{16,24},{24,16},{32,40},{40,32},{48,56},{56,48},{64,72... | collective-permute-start | bytes 276488 | tf_op jit(solution)/shard_map/ppermute | solution.py:234
  18.1 5.0 %collective-permute-start.8 = (f32[2,15,128]{2,1,0:T(8,128)S(1)}, f32[2,15,128]{2,1,0:T(8,128)S(1)}, u32[]{:S(2)}, u32[]{:S(2)}) collective-permute-start(f32[2,15,128]{2,1,0:T(8,128)S(1)} %multiply_add_fusion.6), channel_id=1, source_target_pairs={{0,6},{1,7},{2,4},{3,5},{4,2},{5,3},{6,0},{7,1},{8,14},{9,15},{10,... | collective-permute-start | bytes 46088 | tf_op jit(solution)/shard_map/ppermute | solution.py:234
  23.2 4.4 %collective-permute-start.9 = (f32[15,128]{1,0:T(8,128)S(1)}, f32[15,128]{1,0:T(8,128)S(1)}, u32[]{:S(2)}, u32[]{:S(2)}) collective-permute-start(f32[15,128]{1,0:T(8,128)S(1)} %get-tuple-element.12), channel_id=1, source_target_pairs={{0,7},{1,2},{2,1},{3,4},{4,3},{5,6},{6,5},{7,0},{8,15},{9,10},{10,... | collective-permute-start | bytes 23048 | tf_op jit(solution)/shard_map/ppermute | solution.py:239
  27.7 5.2 %collective-permute-start.1 = (f32[2,15,512]{2,1,0:T(8,128)S(1)}, f32[2,15,512]{2,1,0:T(8,128)S(1)}, u32[]{:S(2)}, u32[]{:S(2)}) collective-permute-start(f32[2,15,512]{2,1,0:T(8,128)S(1)} %multiply_add_fusion.4), channel_id=1, source_target_pairs={{0,16},{8,24},{16,0},{24,8},{32,48},{40,56},{48,32},{56,40},{64,80... | collective-permute-start | bytes 184328 | tf_op jit(solution)/shard_map/ppermute | solution.py:234
  33.0 7.4 %collective-permute-start.2 = (f32[2,15,512]{2,1,0:T(8,128)S(1)}, f32[2,15,512]{2,1,0:T(8,128)S(1)}, u32[]{:S(2)}, u32[]{:S(2)}) collective-permute-start(f32[2,15,512]{2,1,0:T(8,128)S(1)} %multiply_add_fusion.3), channel_id=1, source_target_pairs={{0,56},{8,48},{16,40},{24,32},{32,24},{40,16},{48,8},{56,0},{64,12... | collective-permute-start | bytes 184328 | tf_op jit(solution)/shard_map/ppermute | solution.py:234
  40.4 6.1 %collective-permute-start.3 = (f32[2,15,512]{2,1,0:T(8,128)S(1)}, f32[2,15,512]{2,1,0:T(8,128)S(1)}, u32[]{:S(2)}, u32[]{:S(2)}) collective-permute-start(f32[2,15,512]{2,1,0:T(8,128)S(1)} %multiply_add_fusion.2), channel_id=1, source_target_pairs={{0,64},{8,72},{16,80},{24,88},{32,96},{40,104},{48,112},{56,120},{... | collective-permute-start | bytes 184328 | tf_op jit(solution)/shard_map/ppermute | solution.py:234
  40.6 2.1 %copy-start.1 = (f32[5,3,128,512]{3,2,1,0:T(8,128)S(1)}, f32[5,3,128,512]{3,2,1,0:T(8,128)}, u32[]{:S(2)}) copy-start(f32[5,3,128,512]{3,2,1,0:T(8,128)} %param.11) | copy-start | bytes 11796484
  42.7 9.6 %copy-start.5 = (f32[128,32]{1,0:T(8,128)S(1)}, f32[128,32]{1,0:T(8,128)}, u32[]{:S(2)}) copy-start(f32[128,32]{1,0:T(8,128)} %constant.66.clone.c_ref) | copy-start | bytes 49156
  42.7 9.6 %copy-start.6 = (f32[128,128]{1,0:T(8,128)S(1)}, f32[128,128]{1,0:T(8,128)}, u32[]{:S(2)}) copy-start(f32[128,128]{1,0:T(8,128)} %constant.65.clone.h_ref) | copy-start | bytes 196612
  42.7 9.6 %copy-start.9 = (f32[128]{0:T(128)S(1)}, f32[128]{0:T(128)}, u32[]{:S(2)}) copy-start(f32[128]{0:T(128)} %param.12) | copy-start | bytes 1540
  46.6 5.6 %collective-permute-start.4 = (f32[2,15,512]{2,1,0:T(8,128)S(1)}, f32[2,15,512]{2,1,0:T(8,128)S(1)}, u32[]{:S(2)}, u32[]{:S(2)}) collective-permute-start(f32[2,15,512]{2,1,0:T(8,128)S(1)} %multiply_add_fusion.1), channel_id=1, source_target_pairs={{0,192},{8,200},{16,208},{24,216},{32,224},{40,232},{48,240},{56,2... | collective-permute-start | bytes 184328 | tf_op jit(solution)/shard_map/ppermute | solution.py:234

commit v2 on v1

v2 whole, which is shorter than its diff:
```python
import functools
import math
import numpy as np
import jax
import jax.numpy as jnp
from jax import lax
from jax.experimental import pallas as pl
from jax.experimental.pallas import tpu as pltpu
from jax.sharding import PartitionSpec as P

ALPHA = 0.47
STENCIL_NEAR = (ALPHA + 2.0) / 3.0
STENCIL_FAR = (4.0 * ALPHA - 1.0) / 12.0
ROOT = (math.sqrt(1.0 - 4.0 * ALPHA * ALPHA) - 1.0) / (2.0 * ALPHA)
PEAK = 1.0 / math.sqrt(1.0 - 4.0 * ALPHA * ALPHA)
DECAY = PEAK * (STENCIL_NEAR * (ROOT - 1.0 / ROOT) + STENCIL_FAR * (ROOT**2 - ROOT**-2))
NEXT = PEAK * STENCIL_FAR * (1.0 / ROOT - ROOT)
MASKS_X = ((1, 2, 3), (7,), (8, 16, 24))
MASKS_Y = ((1,), (3,), (7,))
VMEM = 16 * 1024 * 1024
VMEM_FULL = 50 * 1024 * 1024
VMEM_SECOND = 16 * 1024 * 1024
COST_SMALL = pl.CostEstimate(flops=8_000_000, bytes_accessed=8_000_000, transcendentals=0)
COST_FIRST = pl.CostEstimate(flops=3_000_000_000, bytes_accessed=8_000_000, transcendentals=0)
COST_SECOND = pl.CostEstimate(flops=300_000_000, bytes_accessed=8_000_000, transcendentals=0)


def kernel_matrix(extent):
    gap = np.arange(extent)[:, None] - np.arange(extent)[None, :]
    size = np.abs(gap)
    value = DECAY * ROOT ** size.astype(np.float64) + NEXT * (size == 1)
    return np.sign(gap) * value


def border_columns(extent):
    place = np.arange(extent)
    left = DECAY * ROOT ** place.astype(np.float64)
    return np.stack([left, -left[::-1], NEXT * (place == 0), -NEXT * (place == extent - 1)])


def split(value):
    high = value.astype(jnp.bfloat16)
    return high, (value - high.astype(jnp.float32)).astype(jnp.bfloat16)


def dot(left, right):
    return jnp.dot(left, right, preferred_element_type=jnp.float32)


def stacked(rows):
    high = rows.astype(jnp.bfloat16).astype(jnp.float32)
    low = (rows - high).astype(jnp.bfloat16).astype(jnp.float32)
    return jnp.concatenate([high, low, high, jnp.zeros_like(high)], axis=0).astype(jnp.bfloat16)


def row_weights(rows):
    place = lax.broadcasted_iota(jnp.int32, (8, 128), 0)
    down = jnp.zeros((8, 128), jnp.float32)
    up = jnp.zeros((8, 128), jnp.float32)
    for s in range(8):
        down = jnp.where(place == s, ROOT ** (8 - s), down)
        up = jnp.where(place == s, ROOT ** (s + 1), up)
    return down, up


def weighted_sums(load, extent):
    down, up = row_weights(8)
    right = left = None
    for i in range(0, extent, 8):
        rows = load(i)
        right = rows if right is None else right * ROOT**8 + rows
        rows = load(extent - 8 - i)
        left = rows if left is None else left * ROOT**8 + rows
    return jnp.sum(right * down, axis=0, keepdims=True), jnp.sum(left * up, axis=0, keepdims=True)


def first_moments_kernel(u_ref, kept_ref, mx_ref, total_ref, ox_ref, sems):
    even = lax.axis_index("gx") % 2 == 0
    count, extent, width = u_ref.shape
    copies = [pltpu.make_async_copy(u_ref.at[f], kept_ref.at[f], sems.at[f]) for f in range(count)]
    for copy in copies:
        copy.start()
    for f in range(count):
        copies[f].wait()
        pairs = [
            weighted_sums(lambda i: kept_ref[f, i : i + 8, c : c + 128], extent) for c in range(0, width, 128)
        ]
        for k, sums in enumerate(zip(*pairs)):
            row = jnp.concatenate(sums, axis=1)
            mx_ref[k, f : f + 1, :] = row
            total_ref[k, f : f + 1, :] = row
        head = kept_ref[f, 0:1]
        tail = kept_ref[f, extent - 1 : extent]
        mx_ref[2, f : f + 1, :] = jnp.where(even, tail, head)
        ox_ref[f : f + 1, :] = jnp.where(even, head, tail)


def first_moments(cells):
    count, extent, width = cells.shape
    shapes = (cells.shape, (3, count, width), (2, count, width), (count, width))
    return pl.pallas_call(
        first_moments_kernel,
        in_specs=[pl.BlockSpec(memory_space=pl.ANY)],
        out_specs=[pl.BlockSpec(memory_space=pltpu.VMEM)] * 4,
        out_shape=[jax.ShapeDtypeStruct(shape, jnp.float32) for shape in shapes],
        scratch_shapes=[pltpu.SemaphoreType.DMA((count,))],
        compiler_params=pltpu.CompilerParams(vmem_limit_bytes=VMEM_FULL),
        cost_estimate=COST_SMALL,
        name="moments_first",
    )(cells)


def second_moments_kernel(u_ref, after_ref, wx_ref, wy_ref, my_ref, oy_ref, rows_ref):
    even = lax.axis_index("gy") % 2 == 0
    rows_ref[0:1] = wx_ref[pl.ds(lax.axis_index("gx"), 1), :]
    rows_ref[1:2] = wy_ref[pl.ds(lax.axis_index("gy"), 1), :]
    count, extent, width = u_ref.shape
    half = width // 2
    whole = ROOT**half
    for f in range(count):
        turned = [u_ref[f, :, c : c + 128].T for c in range(0, width, 128)]
        sums = []
        for part in range(2):
            piece = lambda i: turned[(part * half + i) // 128][i % 128 : i % 128 + 8]
            sums.extend(weighted_sums(piece, half))
        low, high = turned[0][0:1], turned[-1][127:128]
        rows = [
            sums[2] + whole * sums[0],
            sums[1] + whole * sums[3],
            jnp.where(even, high, low),
        ]
        for k, row in enumerate(rows):
            my_ref[k, f : f + 1, :] = row
        rows = [
            jnp.where(even, low, high),
            sums[0],
            sums[3],
            turned[half // 128 - 1][127:128],
            turned[half // 128][0:1],
        ]
        for k, row in enumerate(rows):
            oy_ref[k, f : f + 1, :] = row


def second_moments(cells, after, table_x, table_y):
    count, extent, width = cells.shape
    return pl.pallas_call(
        second_moments_kernel,
        in_specs=[
            pl.BlockSpec(memory_space=pltpu.VMEM),
            pl.BlockSpec(memory_space=pl.ANY),
            pl.BlockSpec(memory_space=pltpu.VMEM),
            pl.BlockSpec(memory_space=pltpu.VMEM),
        ],
        out_specs=[pl.BlockSpec(memory_space=pltpu.VMEM)] * 3,
        out_shape=[
            jax.ShapeDtypeStruct(shape, jnp.float32) for shape in ((3, count, extent), (5, count, extent), (2, 128))
        ],
        compiler_params=pltpu.CompilerParams(vmem_limit_bytes=VMEM),
        cost_estimate=COST_SMALL,
        name="moments_second",
    )(cells, after, jnp.asarray(table_x), jnp.asarray(table_y))


def first_kernel(u_ref, v_ref, far_ref, near_ref, metric_ref, h_ref, c_ref, out_ref, one_ref, two_ref, done_ref, sems):
    even = lax.axis_index("gx") % 2 == 0
    count, extent, width = u_ref.shape
    row = lax.broadcasted_iota(jnp.int32, (extent, extent), 0)
    column = lax.broadcasted_iota(jnp.int32, (extent, extent), 1)
    metric = jnp.sum(jnp.where(row == column, metric_ref[...], 0.0), axis=1, keepdims=True)
    high, low = split(h_ref[...] * metric)
    one_ref[:, :extent] = high
    one_ref[:, extent:] = high
    two_ref[:, :extent] = low
    scaled = c_ref[...] * metric
    c_high = scaled.astype(jnp.bfloat16).astype(jnp.float32)
    lane = lax.broadcasted_iota(jnp.int32, scaled.shape, 1)
    two_ref[:, extent:] = jnp.where(lane < 16, c_high, scaled - c_high).astype(jnp.bfloat16)
    blank = jnp.zeros((4, width), jnp.float32)
    copies = []
    for f in range(count):
        high, low = split(u_ref[f])
        far, near = far_ref[f : f + 1, :], near_ref[2, f : f + 1, :]
        edges = [jnp.where(even, far, near), jnp.where(even, near, far)]
        rows = jnp.concatenate([v_ref[k, f : f + 1, :] for k in range(2)] + edges + [blank], axis=0)
        total = dot(one_ref[...], jnp.concatenate([high, low], axis=0))
        done_ref[f] = total + dot(two_ref[...], jnp.concatenate([high, stacked(rows)], axis=0))
        copies.append(pltpu.make_async_copy(done_ref.at[f], out_ref.at[f], sems.at[f]))
        copies[-1].start()
    for copy in copies:
        copy.wait()


def first(cells, outside, far, near, metric):
    count, extent, width = cells.shape
    h = kernel_matrix(extent).astype(np.float32)
    c = np.zeros((extent, 32), np.float64)
    columns = border_columns(extent)
    for k in range(3):
        c[:, 8 * k : 8 * k + 4] = columns.T
    return pl.pallas_call(
        first_kernel,
        in_specs=[pl.BlockSpec(memory_space=pltpu.VMEM)] * 7,
        out_specs=pl.BlockSpec(memory_space=pl.ANY),
        out_shape=jax.ShapeDtypeStruct(cells.shape, jnp.float32),
        scratch_shapes=[
            pltpu.VMEM((extent, 2 * extent), jnp.bfloat16),
            pltpu.VMEM((extent, extent + 32), jnp.bfloat16),
            pltpu.VMEM(cells.shape, jnp.float32),
            pltpu.SemaphoreType.DMA((count,)),
        ],
        compiler_params=pltpu.CompilerParams(vmem_limit_bytes=VMEM),
        cost_estimate=COST_FIRST,
        name="slope_first",
    )(cells, outside, far, near, metric.reshape(1, extent), jnp.asarray(h), jnp.asarray(c.astype(np.float32)))


def second_kernel(
    u_ref, outside_ref, own_ref, near_ref, three_ref, seven_ref, metric_ref, h_ref, c_ref, out_ref, done_ref, sems
):
    index = lax.axis_index("gy")
    even = index % 2 == 0
    third = (index + index // 2) % 2 == 1
    count, extent, width = u_ref.shape
    half = width // 2
    ratio = ROOT**half
    copies = []
    for f in range(count):
        left, right = outside_ref[0, f : f + 1, :], outside_ref[1, f : f + 1, :]
        near = near_ref[2, f : f + 1, :]
        far = jnp.where(third, three_ref[2, f : f + 1, :], seven_ref[2, f : f + 1, :])
        rows = stacked(
            jnp.concatenate(
                [
                    left,
                    own_ref[2, f : f + 1, :] + ratio * right,
                    jnp.where(even, far, near),
                    own_ref[4, f : f + 1, :],
                    own_ref[1, f : f + 1, :] + ratio * left,
                    right,
                    own_ref[3, f : f + 1, :],
                    jnp.where(even, near, far),
                ],
                axis=0,
            )
        )
        for part in range(2):
            at = slice(part * half, (part + 1) * half)
            high, low = split(u_ref[f, :, at])
            total = dot(high, h_ref[0]) + dot(low, h_ref[0]) + dot(high, h_ref[1])
            total = total + lax.dot_general(
                rows, c_ref[:, at], (((0,), (0,)), ((), ())), preferred_element_type=jnp.float32
            )
            done_ref[f, :, at] = total * metric_ref[:, at]
        copies.append(pltpu.make_async_copy(done_ref.at[f], out_ref.at[f], sems.at[f]))
        copies[-1].start()
    for copy in copies:
        copy.wait()


def halves(value):
    high = value.astype(np.float32).astype(jnp.bfloat16)
    return high, (value - high.astype(np.float64)).astype(np.float32).astype(jnp.bfloat16)


def second(cells, outside, own, replies, metric):
    count, extent, width = cells.shape
    half = width // 2
    h = np.stack(halves(kernel_matrix(half).T))
    c = np.zeros((8, width), np.float64)
    c[:4, :half] = border_columns(half)
    c[4:, half:] = border_columns(half)
    high, low = halves(c)
    c = np.concatenate([high, high, low, np.zeros_like(high)])
    return pl.pallas_call(
        second_kernel,
        in_specs=[pl.BlockSpec(memory_space=pltpu.VMEM)] * 9,
        out_specs=pl.BlockSpec(memory_space=pl.ANY),
        out_shape=jax.ShapeDtypeStruct(cells.shape, jnp.float32),
        scratch_shapes=[pltpu.VMEM(cells.shape, jnp.float32), pltpu.SemaphoreType.DMA((count,))],
        compiler_params=pltpu.CompilerParams(vmem_limit_bytes=VMEM_SECOND),
        cost_estimate=COST_SECOND,
        name="slope_second",
    )(cells, outside, own, *replies, metric.reshape(1, width), jnp.asarray(h), jnp.asarray(c))


def scan_table(devices, extent, masks):
    ratio = ROOT**extent
    table = np.zeros((devices, 128), np.float64)
    for d in range(devices):
        row = []
        base = 1
        for level in masks:
            size = len(level) + 1
            mine = d // base % size
            place = d % base
            row += [ratio ** (base * (size - 1 - mine)), ratio ** (base * mine)]
            for other in range(1, size):
                theirs = mine ^ other
                row += [ratio ** (base * (size - 1 - theirs)), ratio ** (base * theirs)]
                if theirs < mine:
                    row += [ratio ** (base * (mine - theirs - 1) + place), 0.0]
                else:
                    row += [0.0, ratio ** (base * (theirs - mine) - 1 - place)]
            base *= size
        row += [ratio**d / (1.0 - ratio**devices), ratio ** (devices - 1 - d) / (1.0 - ratio**devices)]
        table[d, : len(row)] = row
    return table.astype(np.float32)


def swap(block, axis, mask):
    return lax.ppermute(block, axis, [(i, i ^ mask) for i in range(lax.axis_size(axis))])


def swap_odd(block, axis):
    count = lax.axis_size(axis)
    return lax.ppermute(block, axis, [(i, (i + (1 if i % 2 else -1)) % count) for i in range(count)])


def after(value, *others):
    return lax.optimization_barrier((value, *others))[0]


def scan_round(row, at, total, outside, replies):
    pair = lambda k: row[k : k + 2][:, None, None]
    grown = pair(at) * total
    at += 2
    for reply in replies:
        grown = grown + pair(at) * reply
        term = pair(at + 2) * reply
        outside = term if outside is None else outside + term
        at += 4
    return at, grown, outside


def shards(fields, metric_first, metric_second):
    fields_count, planes, extent, width = fields.shape
    cells = fields.reshape(fields_count * planes, extent, width)
    cells, message_x, total_x, spare_x = first_moments(cells)
    far_x = swap_odd(spare_x, "gx")
    tables = (
        scan_table(lax.axis_size("gx"), extent, MASKS_X),
        scan_table(lax.axis_size("gy"), width, MASKS_Y),
    )
    message_y, own_y, rows = second_moments(cells, spare_x, *tables)
    message_y = after(message_y, far_x)
    at_x, outside_x = 0, None
    at_y, outside_y, total_y, replies_y = 0, None, message_y[:2], []
    for number, (level_x, level_y) in enumerate(zip(MASKS_X, MASKS_Y)):
        replies = [swap(message_x if number == 0 and mask == 1 else total_x, "gx", mask) for mask in level_x]
        if number == 0:
            near_x = replies[0]
            message = message_y
        else:
            message = after(jnp.concatenate([total_y, own_y[:1]]), total_x)
        (reply,) = [swap(message, "gy", mask) for mask in level_y]
        replies_y.append(reply)
        at_x, total_x, outside_x = scan_round(rows[0], at_x, total_x, outside_x, [r[:2] for r in replies])
        at_y, total_y, outside_y = scan_round(rows[1], at_y, total_y, outside_y, [reply[:2]])
    outside_x = outside_x + rows[0, at_x : at_x + 2][:, None, None] * total_x
    outside_y = outside_y + rows[1, at_y : at_y + 2][:, None, None] * total_y
    slope_second = second(cells, outside_y, own_y, replies_y, metric_second)
    slope_first = first(cells, outside_x, far_x, near_x, metric_first)
    return slope_first.reshape(fields.shape), slope_second.reshape(fields.shape)


def solution(mesh):
    return jax.shard_map(
        shards,
        mesh=mesh,
        in_specs=(P(None, None, "gx", "gy"), P("gx"), P("gy")),
        out_specs=(P(None, None, "gx", "gy"), P(None, None, "gx", "gy")),
        check_vma=False,
    )
```

time: 55.9 us -> 39.4 us (0.70)
  the two profiles are of different devices: /device:TPU:32 before, /device:TPU:1 now
where the time goes in v2:
time: 39.4 us; the launch traced here: 39.3 us
  starting transfers between devices  22.4 us (57%)
  Pallas kernels  8.79 us (22%)
  waiting for transfers between devices  6.58 us (17%)
  between operations  0.83 us (2%)
  other arithmetic  0.54 us (1%)
    ppermute x10, starting transfers between devices, swap(): lax.ppermute(block, axis, [(i, i ^ mask) for i in range(lax.axis_size(axi...  17.1 us
    ppermute x10, waiting for transfers between devices, swap(): lax.ppermute(block, axis, [(i, i ^ mask) for i in range(lax.axis_size(axi...  6.5 us
    ppermute x1, starting transfers between devices, swap_odd(): lax.ppermute(block, axis, [(i, (i + (1 if i % 2 else -1)) % count) for i...  5.33 us
    pallas_call x1, Pallas kernels, second(): pl.pallas_call(second_kernel, in_specs=[pl.BlockSpec(memory_space=pltpu.V...  3.06 us
    pallas_call x1, Pallas kernels, first(): pl.pallas_call(first_kernel, in_specs=[pl.BlockSpec(memory_space=pltpu.VM...  2.34 us
    pallas_call x1, Pallas kernels, first_moments(): pl.pallas_call(first_moments_kernel, in_specs=[pl.BlockSpec(memory_space=...  2.28 us
    pallas_call x1, Pallas kernels, second_moments(): pl.pallas_call(second_moments_kernel, in_specs=[pl.BlockSpec(memory_space...  1.12 us
  transfers between devices with their start and end apart: 11, of which 5 were waited for; matrix products, arithmetic and copies ran while one was open for 1% of the time, Pallas kernels for 11%

profile of v2, /device:TPU:1, one launch (start us, length us, event | category | flops | bytes accessed | tf_op | source)
XLA Modules:
  0.0 39.3 jit_solution(14324892976550696867)
XLA Ops:
  0.6 0.0 copy-start.3
  0.6 0.0 copy-start.2
  0.7 0.0 copy-start
  0.7 0.0 copy-start.1
  0.7 2.3 %moments_first.1 = (f32[15,128,512]{2,1,0:T(8,128)S(1)}, f32[3,15,512]{2,1,0:T(8,128)S(1)}, f32[2,15,512]{2,1,0:T(8,128)S(1)}, f32[15,512]{1,0:T(8,128)S(1)}) custom-call(f32[15,128,512]{2,1,0:T(8,128)} %bitcast.64), custom_call_target="tpu_custom_call" | custom-call | flops 8000000 | bytes 8000000 | tf_op jit(solution)/shard_map/moments_first/pallas_call | solution.py:101
  3.0 5.3 %collective-permute-start.2 = (f32[2,15,512]{2,1,0:T(8,128)S(1)}, f32[2,15,512]{2,1,0:T(8,128)S(1)}, u32[]{:S(2)}, u32[]{:S(2)}) collective-permute-start(f32[2,15,512]{2,1,0:T(8,128)S(1)} %get-tuple-element.16), channel_id=1, source_target_pairs={{0,24},{8,16},{16,8},{24,0},{32,56},{40,48},{48,40},{56,32},{64,88... | collective-permute-start | bytes 184328 | tf_op jit(solution)/shard_map/ppermute | solution.py:312
  8.2 5.3 %collective-permute-start.7 = (f32[15,512]{1,0:T(8,128)S(1)}, f32[15,512]{1,0:T(8,128)S(1)}, u32[]{:S(2)}, u32[]{:S(2)}) collective-permute-start(f32[15,512]{1,0:T(8,128)S(1)} %get-tuple-element.13.after_ref), channel_id=1, source_target_pairs={{0,248},{8,16},{16,8},{24,32},{32,24},{40,48},{48,40},{56,64},{64,... | collective-permute-start | bytes 92168 | tf_op jit(solution)/shard_map/ppermute | solution.py:317
  13.6 1.1 %moments_second.1 = (f32[3,15,128]{2,1,0:T(8,128)S(1)}, f32[5,15,128]{2,1,0:T(8,128)S(1)}, f32[2,128]{1,0:T(2,128)S(1)}) custom-call(f32[15,128,512]{2,1,0:T(8,128)S(1)} %get-tuple-element.12.u_ref, f32[15,512]{1,0:T(8,128)S(1)} %get-tuple-element.13.after_ref, f32[32,128]{1,0:T(8,128)S(1)} %copy-done.2, f32[8,128]{1,0:T(8,128)S(1)} %copy-done.3), custom_call_target="tpu_custom_call" | custom-call | flops 8000000 | bytes 8000000 | tf_op jit(solution)/shard_map/moments_second/pallas_call | solution.py:147
  14.7 0.1 slice_bitcast_fusion.9
  14.8 0.1 collective-permute-done.7.far_ref
  14.9 2.1 %collective-permute-start.8 = (f32[3,15,128]{2,1,0:T(8,128)S(1)}, f32[3,15,128]{2,1,0:T(8,128)S(1)}, u32[]{:S(2)}, u32[]{:S(2)}) collective-permute-start(f32[3,15,128]{2,1,0:T(8,128)S(1)} %get-tuple-element.18), channel_id=1, source_target_pairs={{0,1},{1,0},{2,3},{3,2},{4,5},{5,4},{6,7},{7,6},{8,9},{9,8},{10,11... | collective-permute-start | bytes 69128 | tf_op jit(solution)/shard_map/ppermute | solution.py:312
  17.0 0.1 slice_bitcast_fusion.27
  17.1 0.8 %collective-permute-done.8.near_ref = f32[3,15,128]{2,1,0:T(8,128)S(1)} collective-permute-done((f32[3,15,128]{2,1,0:T(8,128)S(1)}, f32[3,15,128]{2,1,0:T(8,128)S(1)}, u32[]{:S(2)}, u32[]{:S(2)}) %collective-permute-start.8) | collective-permute-done | bytes 23072 | tf_op jit(solution)/shard_map/ppermute | solution.py:312
  17.8 0.1 multiply_add_fusion.5
  17.9 0.1 multiply_add_fusion.2
  18.0 3.0 %collective-permute-start.9 = (f32[3,15,128]{2,1,0:T(8,128)S(1)}, f32[3,15,128]{2,1,0:T(8,128)S(1)}, u32[]{:S(2)}, u32[]{:S(2)}) collective-permute-start(f32[3,15,128]{2,1,0:T(8,128)S(1)} %pad_maximum_fusion.1), channel_id=1, source_target_pairs={{0,3},{1,2},{2,1},{3,0},{4,7},{5,6},{6,5},{7,4},{8,11},{9,10},{10,... | collective-permute-start | bytes 69128 | tf_op jit(solution)/shard_map/ppermute | solution.py:312
  21.1 0.2 collective-permute-start.3
  21.3 1.6 %collective-permute-done.9.three_ref = f32[3,15,128]{2,1,0:T(8,128)S(1)} collective-permute-done((f32[3,15,128]{2,1,0:T(8,128)S(1)}, f32[3,15,128]{2,1,0:T(8,128)S(1)}, u32[]{:S(2)}, u32[]{:S(2)}) %collective-permute-start.9) | collective-permute-done | bytes 23072 | tf_op jit(solution)/shard_map/ppermute | solution.py:312
  22.9 0.1 multiply_add_fusion.4
  23.0 3.9 %collective-permute-done.3 = f32[2,15,512]{2,1,0:T(8,128)S(1)} collective-permute-done((f32[2,15,512]{2,1,0:T(8,128)S(1)}, f32[2,15,512]{2,1,0:T(8,128)S(1)}, u32[]{:S(2)}, u32[]{:S(2)}) %collective-permute-start.3) | collective-permute-done | bytes 61472 | tf_op jit(solution)/shard_map/ppermute | solution.py:312
  26.9 0.1 multiply_add_fusion.1
  27.0 3.2 %collective-permute-start.10 = (f32[3,15,128]{2,1,0:T(8,128)S(1)}, f32[3,15,128]{2,1,0:T(8,128)S(1)}, u32[]{:S(2)}, u32[]{:S(2)}) collective-permute-start(f32[3,15,128]{2,1,0:T(8,128)S(1)} %pad_maximum_fusion), channel_id=1, source_target_pairs={{0,7},{1,6},{2,5},{3,4},{4,3},{5,2},{6,1},{7,0},{8,15},{9,14},{10,... | collective-permute-start | bytes 69128 | tf_op jit(solution)/shard_map/ppermute | solution.py:312
  30.1 1.2 %collective-permute-start.6 = (f32[2,15,512]{2,1,0:T(8,128)S(1)}, f32[2,15,512]{2,1,0:T(8,128)S(1)}, u32[]{:S(2)}, u32[]{:S(2)}) collective-permute-start(f32[2,15,512]{2,1,0:T(8,128)S(1)} %multiply_add_fusion.1), channel_id=1, source_target_pairs={{0,192},{8,200},{16,208},{24,216},{32,224},{40,232},{48,240},{56,2... | collective-permute-start | bytes 184328 | tf_op jit(solution)/shard_map/ppermute | solution.py:312
  31.3 2.1 %collective-permute-start.4 = (f32[2,15,512]{2,1,0:T(8,128)S(1)}, f32[2,15,512]{2,1,0:T(8,128)S(1)}, u32[]{:S(2)}, u32[]{:S(2)}) collective-permute-start(f32[2,15,512]{2,1,0:T(8,128)S(1)} %multiply_add_fusion.1), channel_id=1, source_target_pairs={{0,64},{8,72},{16,80},{24,88},{32,96},{40,104},{48,112},{56,120},{... | collective-permute-start | bytes 184328 | tf_op jit(solution)/shard_map/ppermute | solution.py:312
  33.4 0.1 multiply_add_fusion.3.outside_ref
  33.5 0.0 copy-start.5
  33.5 0.0 copy-start.6
  33.5 0.0 copy-start.7
  33.5 3.1 %slope_second.1 = f32[15,128,512]{2,1,0:T(8,128)} custom-call(f32[15,128,512]{2,1,0:T(8,128)S(1)} %get-tuple-element.12.u_ref, f32[2,15,128]{2,1,0:T(8,128)S(1)} %multiply_add_fusion.3.outside_ref, f32[5,15,128]{2,1,0:T(8,128)S(1)} %get-tuple-element.19.own_ref, f32[3,15,128]{2,1,0:T(8,128)S(1)} %collective-permute-done.8.near_ref, ...), custom_call_target="tpu_custom_call" | custom-call | flops 300000000 | bytes 8000000 | tf_op jit(solution)/shard_map/slope_second/pallas_call | solution.py:275
  36.6 0.2 collective-permute-done.4
  36.9 0.1 multiply_add_fusion.v_ref
  37.0 2.3 %slope_first.1 = f32[15,128,512]{2,1,0:T(8,128)} custom-call(f32[15,128,512]{2,1,0:T(8,128)S(1)} %get-tuple-element.12.u_ref, f32[2,15,512]{2,1,0:T(8,128)S(1)} %multiply_add_fusion.v_ref, f32[15,512]{1,0:T(8,128)S(1)} %collective-permute-done.7.far_ref, f32[3,15,512]{2,1,0:T(8,128)S(1)} %collective-permute-done.near_ref, f32[1,128]{1,0:T(1,128)S(1)} %bitcast.62, ...), custom_call_target="tpu_custom_call" | custom-call | flops 3000000000 | bytes 8000000 | tf_op jit(solution)/shard_map/slope_first/pallas_call | solution.py:201
  (21 shorter events, 0.1 us)
Async XLA Ops:
  0.6 12.9 %copy-start.3 = (f32[8,128]{1,0:T(8,128)S(1)}, f32[8,128]{1,0:T(8,128)}, u32[]{:S(2)}) copy-start(f32[8,128]{1,0:T(8,128)} %constant.13.clone.wy_ref) | copy-start | bytes 12292
  0.6 12.9 %copy-start.2 = (f32[32,128]{1,0:T(8,128)S(1)}, f32[32,128]{1,0:T(8,128)}, u32[]{:S(2)}) copy-start(f32[32,128]{1,0:T(8,128)} %constant.12.clone.wx_ref) | copy-start | bytes 49156
  0.7 32.8 %copy-start = (bf16[2,256,256]{2,1,0:T(8,128)(2,1)S(1)}, bf16[2,256,256]{2,1,0:T(8,128)(2,1)}, u32[]{:S(2)}) copy-start(bf16[2,256,256]{2,1,0:T(8,128)(2,1)} %constant.14.clone.h_ref) | copy-start | bytes 786436
  0.7 32.8 %copy-start.1 = (bf16[32,512]{1,0:T(8,128)(2,1)S(1)}, bf16[32,512]{1,0:T(8,128)(2,1)}, u32[]{:S(2)}) copy-start(bf16[32,512]{1,0:T(8,128)(2,1)} %constant.15.clone.c_ref) | copy-start | bytes 98308
  0.7 32.8 %copy-start.4 = (f32[512]{0:T(512)S(1)}, f32[512]{0:T(512)}, u32[]{:S(2)}) copy-start(f32[512]{0:T(512)} %param.11) | copy-start | bytes 6148
  3.0 14.9 %collective-permute-start.2 = (f32[2,15,512]{2,1,0:T(8,128)S(1)}, f32[2,15,512]{2,1,0:T(8,128)S(1)}, u32[]{:S(2)}, u32[]{:S(2)}) collective-permute-start(f32[2,15,512]{2,1,0:T(8,128)S(1)} %get-tuple-element.16), channel_id=1, source_target_pairs={{0,24},{8,16},{16,8},{24,0},{32,56},{40,48},{48,40},{56,32},{64,88... | collective-permute-start | bytes 184328 | tf_op jit(solution)/shard_map/ppermute | solution.py:312
  8.2 9.7 %collective-permute-start.1 = (f32[2,15,512]{2,1,0:T(8,128)S(1)}, f32[2,15,512]{2,1,0:T(8,128)S(1)}, u32[]{:S(2)}, u32[]{:S(2)}) collective-permute-start(f32[2,15,512]{2,1,0:T(8,128)S(1)} %get-tuple-element.16), channel_id=1, source_target_pairs={{0,16},{8,24},{16,0},{24,8},{32,48},{40,56},{48,32},{56,40},{64,80... | collective-permute-start | bytes 184328 | tf_op jit(solution)/shard_map/ppermute | solution.py:312
  8.2 6.6 %collective-permute-start.7 = (f32[15,512]{1,0:T(8,128)S(1)}, f32[15,512]{1,0:T(8,128)S(1)}, u32[]{:S(2)}, u32[]{:S(2)}) collective-permute-start(f32[15,512]{1,0:T(8,128)S(1)} %get-tuple-element.13.after_ref), channel_id=1, source_target_pairs={{0,248},{8,16},{16,8},{24,32},{32,24},{40,48},{48,40},{56,64},{64,... | collective-permute-start | bytes 92168 | tf_op jit(solution)/shard_map/ppermute | solution.py:317
  13.6 4.4 %collective-permute-start = (f32[3,15,512]{2,1,0:T(8,128)S(1)}, f32[3,15,512]{2,1,0:T(8,128)S(1)}, u32[]{:S(2)}, u32[]{:S(2)}) collective-permute-start(f32[3,15,512]{2,1,0:T(8,128)S(1)} %get-tuple-element.15), channel_id=1, source_target_pairs={{0,8},{8,0},{16,24},{24,16},{32,40},{40,32},{48,56},{56,48},{64,72... | collective-permute-start | bytes 276488 | tf_op jit(solution)/shard_map/ppermute | solution.py:312
  14.9 3.0 %collective-permute-start.8 = (f32[3,15,128]{2,1,0:T(8,128)S(1)}, f32[3,15,128]{2,1,0:T(8,128)S(1)}, u32[]{:S(2)}, u32[]{:S(2)}) collective-permute-start(f32[3,15,128]{2,1,0:T(8,128)S(1)} %get-tuple-element.18), channel_id=1, source_target_pairs={{0,1},{1,0},{2,3},{3,2},{4,5},{5,4},{6,7},{7,6},{8,9},{9,8},{10,11... | collective-permute-start | bytes 69128 | tf_op jit(solution)/shard_map/ppermute | solution.py:312
  18.0 4.8 %collective-permute-start.9 = (f32[3,15,128]{2,1,0:T(8,128)S(1)}, f32[3,15,128]{2,1,0:T(8,128)S(1)}, u32[]{:S(2)}, u32[]{:S(2)}) collective-permute-start(f32[3,15,128]{2,1,0:T(8,128)S(1)} %pad_maximum_fusion.1), channel_id=1, source_target_pairs={{0,3},{1,2},{2,1},{3,0},{4,7},{5,6},{6,5},{7,4},{8,11},{9,10},{10,... | collective-permute-start | bytes 69128 | tf_op jit(solution)/shard_map/ppermute | solution.py:312
  21.1 5.8 %collective-permute-start.3 = (f32[2,15,512]{2,1,0:T(8,128)S(1)}, f32[2,15,512]{2,1,0:T(8,128)S(1)}, u32[]{:S(2)}, u32[]{:S(2)}) collective-permute-start(f32[2,15,512]{2,1,0:T(8,128)S(1)} %multiply_add_fusion.2), channel_id=1, source_target_pairs={{0,56},{8,48},{16,40},{24,32},{32,24},{40,16},{48,8},{56,0},{64,12... | collective-permute-start | bytes 184328 | tf_op jit(solution)/shard_map/ppermute | solution.py:312
  27.0 6.4 %collective-permute-start.10 = (f32[3,15,128]{2,1,0:T(8,128)S(1)}, f32[3,15,128]{2,1,0:T(8,128)S(1)}, u32[]{:S(2)}, u32[]{:S(2)}) collective-permute-start(f32[3,15,128]{2,1,0:T(8,128)S(1)} %pad_maximum_fusion), channel_id=1, source_target_pairs={{0,7},{1,6},{2,5},{3,4},{4,3},{5,2},{6,1},{7,0},{8,15},{9,14},{10,... | collective-permute-start | bytes 69128 | tf_op jit(solution)/shard_map/ppermute | solution.py:312
  30.1 6.5 %collective-permute-start.6 = (f32[2,15,512]{2,1,0:T(8,128)S(1)}, f32[2,15,512]{2,1,0:T(8,128)S(1)}, u32[]{:S(2)}, u32[]{:S(2)}) collective-permute-start(f32[2,15,512]{2,1,0:T(8,128)S(1)} %multiply_add_fusion.1), channel_id=1, source_target_pairs={{0,192},{8,200},{16,208},{24,216},{32,224},{40,232},{48,240},{56,2... | collective-permute-start | bytes 184328 | tf_op jit(solution)/shard_map/ppermute | solution.py:312
  31.3 5.3 %collective-permute-start.5 = (f32[2,15,512]{2,1,0:T(8,128)S(1)}, f32[2,15,512]{2,1,0:T(8,128)S(1)}, u32[]{:S(2)}, u32[]{:S(2)}) collective-permute-start(f32[2,15,512]{2,1,0:T(8,128)S(1)} %multiply_add_fusion.1), channel_id=1, source_target_pairs={{0,128},{8,136},{16,144},{24,152},{32,160},{40,168},{48,176},{56,1... | collective-permute-start | bytes 184328 | tf_op jit(solution)/shard_map/ppermute | solution.py:312
  31.3 5.5 %collective-permute-start.4 = (f32[2,15,512]{2,1,0:T(8,128)S(1)}, f32[2,15,512]{2,1,0:T(8,128)S(1)}, u32[]{:S(2)}, u32[]{:S(2)}) collective-permute-start(f32[2,15,512]{2,1,0:T(8,128)S(1)} %multiply_add_fusion.1), channel_id=1, source_target_pairs={{0,64},{8,72},{16,80},{24,88},{32,96},{40,104},{48,112},{56,120},{... | collective-permute-start | bytes 184328 | tf_op jit(solution)/shard_map/ppermute | solution.py:312
  33.5 3.5 %copy-start.5 = (f32[128]{0:T(128)S(1)}, f32[128]{0:T(128)}, u32[]{:S(2)}) copy-start(f32[128]{0:T(128)} %param.10) | copy-start | bytes 1540
  33.5 3.5 %copy-start.6 = (f32[128,32]{1,0:T(8,128)S(1)}, f32[128,32]{1,0:T(8,128)}, u32[]{:S(2)}) copy-start(f32[128,32]{1,0:T(8,128)} %constant.17.clone.c_ref) | copy-start | bytes 49156
  33.5 3.5 %copy-start.7 = (f32[128,128]{1,0:T(8,128)S(1)}, f32[128,128]{1,0:T(8,128)}, u32[]{:S(2)}) copy-start(f32[128,128]{1,0:T(8,128)} %constant.16.clone.h_ref) | copy-start | bytes 196612

commit v3 on v2

--- a/solution.py
+++ b/solution.py
@@ -356,6 +356,9 @@
         (reply,) = [swap(message, "gy", mask) for mask in level_y]
         replies_y.append(reply)
         at_x, total_x, outside_x = scan_round(rows[0], at_x, total_x, outside_x, [r[:2] for r in replies])
+        if number == 1:
+            reply = after(reply, total_x)
+            replies_y[-1] = reply
         at_y, total_y, outside_y = scan_round(rows[1], at_y, total_y, outside_y, [reply[:2]])
     outside_x = outside_x + rows[0, at_x : at_x + 2][:, None, None] * total_x
     outside_y = outside_y + rows[1, at_y : at_y + 2][:, None, None] * total_y

time: 39.4 us -> 38.5 us (0.977)
  waiting for transfers between devices: 6.58 us -> 2.81 us
  starting transfers between devices: 22.4 us -> 25.2 us
    ppermute x10, waiting for transfers between devices: 6.5 us -> 2.73 us  [swap(): lax.ppermute(block, axis, [(i, i ^ mask) for i in range(lax.axis_size(axi...]
    ppermute x10, starting transfers between devices: 17.1 us -> 19.9 us  [swap(): lax.ppermute(block, axis, [(i, i ^ mask) for i in range(lax.axis_size(axi...]
where the time goes in v3:
time: 38.5 us; the launch traced here: 38.4 us
  starting transfers between devices  25.2 us (65%)
  Pallas kernels  8.79 us (23%)
  waiting for transfers between devices  2.81 us (7%)
  between operations  0.82 us (2%)
  other arithmetic  0.53 us (1%)
    ppermute x10, starting transfers between devices, swap(): lax.ppermute(block, axis, [(i, i ^ mask) for i in range(lax.axis_size(axi...  19.9 us
    ppermute x1, starting transfers between devices, swap_odd(): lax.ppermute(block, axis, [(i, (i + (1 if i % 2 else -1)) % count) for i...  5.33 us
    pallas_call x1, Pallas kernels, second(): pl.pallas_call(second_kernel, in_specs=[pl.BlockSpec(memory_space=pltpu.V...  3.06 us
    ppermute x10, waiting for transfers between devices, swap(): lax.ppermute(block, axis, [(i, i ^ mask) for i in range(lax.axis_size(axi...  2.73 us
    pallas_call x1, Pallas kernels, first(): pl.pallas_call(first_kernel, in_specs=[pl.BlockSpec(memory_space=pltpu.VM...  2.34 us
    pallas_call x1, Pallas kernels, first_moments(): pl.pallas_call(first_moments_kernel, in_specs=[pl.BlockSpec(memory_space=...  2.28 us
    pallas_call x1, Pallas kernels, second_moments(): pl.pallas_call(second_moments_kernel, in_specs=[pl.BlockSpec(memory_space...  1.12 us
  transfers between devices with their start and end apart: 11, of which 5 were waited for; matrix products, arithmetic and copies ran while one was open for 1% of the time, Pallas kernels for 11%

profile of v3, /device:TPU:1, one launch (start us, length us, event | category | flops | bytes accessed | tf_op | source)
XLA Modules:
  0.0 38.4 jit_solution(15528391157601020326)
XLA Ops:
  0.6 0.0 copy-start.3
  0.6 0.0 copy-start.2
  0.7 0.0 copy-start
  0.7 0.0 copy-start.1
  0.7 2.3 %moments_first.1 = (f32[15,128,512]{2,1,0:T(8,128)S(1)}, f32[3,15,512]{2,1,0:T(8,128)S(1)}, f32[2,15,512]{2,1,0:T(8,128)S(1)}, f32[15,512]{1,0:T(8,128)S(1)}) custom-call(f32[15,128,512]{2,1,0:T(8,128)} %bitcast.64), custom_call_target="tpu_custom_call" | custom-call | flops 8000000 | bytes 8000000 | tf_op jit(solution)/shard_map/moments_first/pallas_call | solution.py:101
  3.0 5.3 %collective-permute-start.2 = (f32[2,15,512]{2,1,0:T(8,128)S(1)}, f32[2,15,512]{2,1,0:T(8,128)S(1)}, u32[]{:S(2)}, u32[]{:S(2)}) collective-permute-start(f32[2,15,512]{2,1,0:T(8,128)S(1)} %get-tuple-element.17), channel_id=1, source_target_pairs={{0,24},{8,16},{16,8},{24,0},{32,56},{40,48},{48,40},{56,32},{64,88... | collective-permute-start | bytes 184328 | tf_op jit(solution)/shard_map/ppermute | solution.py:312
  8.2 5.3 %collective-permute-start.7 = (f32[15,512]{1,0:T(8,128)S(1)}, f32[15,512]{1,0:T(8,128)S(1)}, u32[]{:S(2)}, u32[]{:S(2)}) collective-permute-start(f32[15,512]{1,0:T(8,128)S(1)} %get-tuple-element.14.after_ref), channel_id=1, source_target_pairs={{0,248},{8,16},{16,8},{24,32},{32,24},{40,48},{48,40},{56,64},{64,... | collective-permute-start | bytes 92168 | tf_op jit(solution)/shard_map/ppermute | solution.py:317
  13.6 1.1 %moments_second.1 = (f32[3,15,128]{2,1,0:T(8,128)S(1)}, f32[5,15,128]{2,1,0:T(8,128)S(1)}, f32[2,128]{1,0:T(2,128)S(1)}) custom-call(f32[15,128,512]{2,1,0:T(8,128)S(1)} %get-tuple-element.13.u_ref, f32[15,512]{1,0:T(8,128)S(1)} %get-tuple-element.14.after_ref, f32[32,128]{1,0:T(8,128)S(1)} %copy-done.2, f32[8,128]{1,0:T(8,128)S(1)} %copy-done.3), custom_call_target="tpu_custom_call" | custom-call | flops 8000000 | bytes 8000000 | tf_op jit(solution)/shard_map/moments_second/pallas_call | solution.py:147
  14.7 0.1 slice_bitcast_fusion.9
  14.8 0.1 collective-permute-done.7.far_ref
  14.9 2.1 %collective-permute-start.8 = (f32[3,15,128]{2,1,0:T(8,128)S(1)}, f32[3,15,128]{2,1,0:T(8,128)S(1)}, u32[]{:S(2)}, u32[]{:S(2)}) collective-permute-start(f32[3,15,128]{2,1,0:T(8,128)S(1)} %get-tuple-element.19), channel_id=1, source_target_pairs={{0,1},{1,0},{2,3},{3,2},{4,5},{5,4},{6,7},{7,6},{8,9},{9,8},{10,11... | collective-permute-start | bytes 69128 | tf_op jit(solution)/shard_map/ppermute | solution.py:312
  17.0 0.1 slice_bitcast_fusion.27
  17.1 0.8 %collective-permute-done.8.near_ref = f32[3,15,128]{2,1,0:T(8,128)S(1)} collective-permute-done((f32[3,15,128]{2,1,0:T(8,128)S(1)}, f32[3,15,128]{2,1,0:T(8,128)S(1)}, u32[]{:S(2)}, u32[]{:S(2)}) %collective-permute-start.8) | collective-permute-done | bytes 23072 | tf_op jit(solution)/shard_map/ppermute | solution.py:312
  17.8 0.1 multiply_add_fusion.5
  17.9 0.1 multiply_add_fusion.2
  18.0 1.7 %collective-permute-start.3 = (f32[2,15,512]{2,1,0:T(8,128)S(1)}, f32[2,15,512]{2,1,0:T(8,128)S(1)}, u32[]{:S(2)}, u32[]{:S(2)}) collective-permute-start(f32[2,15,512]{2,1,0:T(8,128)S(1)} %multiply_add_fusion.2), channel_id=1, source_target_pairs={{0,56},{8,48},{16,40},{24,32},{32,24},{40,16},{48,8},{56,0},{64,12... | collective-permute-start | bytes 184328 | tf_op jit(solution)/shard_map/ppermute | solution.py:312
  19.8 1.8 %collective-permute-start.9 = (f32[3,15,128]{2,1,0:T(8,128)S(1)}, f32[3,15,128]{2,1,0:T(8,128)S(1)}, u32[]{:S(2)}, u32[]{:S(2)}) collective-permute-start(f32[3,15,128]{2,1,0:T(8,128)S(1)} %pad_maximum_fusion.1), channel_id=1, source_target_pairs={{0,3},{1,2},{2,1},{3,0},{4,7},{5,6},{6,5},{7,4},{8,11},{9,10},{10,... | collective-permute-start | bytes 69128 | tf_op jit(solution)/shard_map/ppermute | solution.py:312
  21.6 0.9 %collective-permute-done.3 = f32[2,15,512]{2,1,0:T(8,128)S(1)} collective-permute-done((f32[2,15,512]{2,1,0:T(8,128)S(1)}, f32[2,15,512]{2,1,0:T(8,128)S(1)}, u32[]{:S(2)}, u32[]{:S(2)}) %collective-permute-start.3) | collective-permute-done | bytes 61472 | tf_op jit(solution)/shard_map/ppermute | solution.py:312
  22.4 0.1 multiply_add_fusion.1
  22.5 0.9 %collective-permute-done.9.three_ref = f32[3,15,128]{2,1,0:T(8,128)S(1)} collective-permute-done((f32[3,15,128]{2,1,0:T(8,128)S(1)}, f32[3,15,128]{2,1,0:T(8,128)S(1)}, u32[]{:S(2)}, u32[]{:S(2)}) %collective-permute-start.9) | collective-permute-done | bytes 23072 | tf_op jit(solution)/shard_map/ppermute | solution.py:312
  23.4 0.1 multiply_add_fusion.4
  23.5 5.7 %collective-permute-start.10 = (f32[3,15,128]{2,1,0:T(8,128)S(1)}, f32[3,15,128]{2,1,0:T(8,128)S(1)}, u32[]{:S(2)}, u32[]{:S(2)}) collective-permute-start(f32[3,15,128]{2,1,0:T(8,128)S(1)} %pad_maximum_fusion), channel_id=1, source_target_pairs={{0,7},{1,6},{2,5},{3,4},{4,3},{5,2},{6,1},{7,0},{8,15},{9,14},{10,... | collective-permute-start | bytes 69128 | tf_op jit(solution)/shard_map/ppermute | solution.py:312
  29.2 1.5 %collective-permute-start.6 = (f32[2,15,512]{2,1,0:T(8,128)S(1)}, f32[2,15,512]{2,1,0:T(8,128)S(1)}, u32[]{:S(2)}, u32[]{:S(2)}) collective-permute-start(f32[2,15,512]{2,1,0:T(8,128)S(1)} %multiply_add_fusion.1), channel_id=1, source_target_pairs={{0,192},{8,200},{16,208},{24,216},{32,224},{40,232},{48,240},{56,2... | collective-permute-start | bytes 184328 | tf_op jit(solution)/shard_map/ppermute | solution.py:312
  30.7 1.7 %collective-permute-start.4 = (f32[2,15,512]{2,1,0:T(8,128)S(1)}, f32[2,15,512]{2,1,0:T(8,128)S(1)}, u32[]{:S(2)}, u32[]{:S(2)}) collective-permute-start(f32[2,15,512]{2,1,0:T(8,128)S(1)} %multiply_add_fusion.1), channel_id=1, source_target_pairs={{0,64},{8,72},{16,80},{24,88},{32,96},{40,104},{48,112},{56,120},{... | collective-permute-start | bytes 184328 | tf_op jit(solution)/shard_map/ppermute | solution.py:312
  32.4 0.1 multiply_add_fusion.3.outside_ref
  32.5 0.0 copy-start.5
  32.6 0.0 copy-start.6
  32.6 0.0 copy-start.7
  32.6 3.1 %slope_second.1 = f32[15,128,512]{2,1,0:T(8,128)} custom-call(f32[15,128,512]{2,1,0:T(8,128)S(1)} %get-tuple-element.13.u_ref, f32[2,15,128]{2,1,0:T(8,128)S(1)} %multiply_add_fusion.3.outside_ref, f32[5,15,128]{2,1,0:T(8,128)S(1)} %get-tuple-element.20.own_ref, f32[3,15,128]{2,1,0:T(8,128)S(1)} %collective-permute-done.8.near_ref, ...), custom_call_target="tpu_custom_call" | custom-call | flops 300000000 | bytes 8000000 | tf_op jit(solution)/shard_map/slope_second/pallas_call | solution.py:275
  35.7 0.2 collective-permute-done.4
  35.9 0.1 multiply_add_fusion.v_ref
  36.0 2.3 %slope_first.1 = f32[15,128,512]{2,1,0:T(8,128)} custom-call(f32[15,128,512]{2,1,0:T(8,128)S(1)} %get-tuple-element.13.u_ref, f32[2,15,512]{2,1,0:T(8,128)S(1)} %multiply_add_fusion.v_ref, f32[15,512]{1,0:T(8,128)S(1)} %collective-permute-done.7.far_ref, f32[3,15,512]{2,1,0:T(8,128)S(1)} %collective-permute-done.near_ref, f32[1,128]{1,0:T(1,128)S(1)} %bitcast.62, ...), custom_call_target="tpu_custom_call" | custom-call | flops 3000000000 | bytes 8000000 | tf_op jit(solution)/shard_map/slope_first/pallas_call | solution.py:201
  (21 shorter events, 0.1 us)
Async XLA Ops:
  0.6 12.9 %copy-start.3 = (f32[8,128]{1,0:T(8,128)S(1)}, f32[8,128]{1,0:T(8,128)}, u32[]{:S(2)}) copy-start(f32[8,128]{1,0:T(8,128)} %constant.13.clone.wy_ref) | copy-start | bytes 12292
  0.6 12.9 %copy-start.2 = (f32[32,128]{1,0:T(8,128)S(1)}, f32[32,128]{1,0:T(8,128)}, u32[]{:S(2)}) copy-start(f32[32,128]{1,0:T(8,128)} %constant.12.clone.wx_ref) | copy-start | bytes 49156
  0.7 31.9 %copy-start = (bf16[2,256,256]{2,1,0:T(8,128)(2,1)S(1)}, bf16[2,256,256]{2,1,0:T(8,128)(2,1)}, u32[]{:S(2)}) copy-start(bf16[2,256,256]{2,1,0:T(8,128)(2,1)} %constant.14.clone.h_ref) | copy-start | bytes 786436
  0.7 31.9 %copy-start.1 = (bf16[32,512]{1,0:T(8,128)(2,1)S(1)}, bf16[32,512]{1,0:T(8,128)(2,1)}, u32[]{:S(2)}) copy-start(bf16[32,512]{1,0:T(8,128)(2,1)} %constant.15.clone.c_ref) | copy-start | bytes 98308
  0.7 31.9 %copy-start.4 = (f32[512]{0:T(512)S(1)}, f32[512]{0:T(512)}, u32[]{:S(2)}) copy-start(f32[512]{0:T(512)} %param.11) | copy-start | bytes 6148
  3.0 14.9 %collective-permute-start.2 = (f32[2,15,512]{2,1,0:T(8,128)S(1)}, f32[2,15,512]{2,1,0:T(8,128)S(1)}, u32[]{:S(2)}, u32[]{:S(2)}) collective-permute-start(f32[2,15,512]{2,1,0:T(8,128)S(1)} %get-tuple-element.17), channel_id=1, source_target_pairs={{0,24},{8,16},{16,8},{24,0},{32,56},{40,48},{48,40},{56,32},{64,88... | collective-permute-start | bytes 184328 | tf_op jit(solution)/shard_map/ppermute | solution.py:312
  8.2 9.7 %collective-permute-start.1 = (f32[2,15,512]{2,1,0:T(8,128)S(1)}, f32[2,15,512]{2,1,0:T(8,128)S(1)}, u32[]{:S(2)}, u32[]{:S(2)}) collective-permute-start(f32[2,15,512]{2,1,0:T(8,128)S(1)} %get-tuple-element.17), channel_id=1, source_target_pairs={{0,16},{8,24},{16,0},{24,8},{32,48},{40,56},{48,32},{56,40},{64,80... | collective-permute-start | bytes 184328 | tf_op jit(solution)/shard_map/ppermute | solution.py:312
  8.2 6.6 %collective-permute-start.7 = (f32[15,512]{1,0:T(8,128)S(1)}, f32[15,512]{1,0:T(8,128)S(1)}, u32[]{:S(2)}, u32[]{:S(2)}) collective-permute-start(f32[15,512]{1,0:T(8,128)S(1)} %get-tuple-element.14.after_ref), channel_id=1, source_target_pairs={{0,248},{8,16},{16,8},{24,32},{32,24},{40,48},{48,40},{56,64},{64,... | collective-permute-start | bytes 92168 | tf_op jit(solution)/shard_map/ppermute | solution.py:317
  13.6 4.3 %collective-permute-start = (f32[3,15,512]{2,1,0:T(8,128)S(1)}, f32[3,15,512]{2,1,0:T(8,128)S(1)}, u32[]{:S(2)}, u32[]{:S(2)}) collective-permute-start(f32[3,15,512]{2,1,0:T(8,128)S(1)} %get-tuple-element.16), channel_id=1, source_target_pairs={{0,8},{8,0},{16,24},{24,16},{32,40},{40,32},{48,56},{56,48},{64,72... | collective-permute-start | bytes 276488 | tf_op jit(solution)/shard_map/ppermute | solution.py:312
  14.9 3.0 %collective-permute-start.8 = (f32[3,15,128]{2,1,0:T(8,128)S(1)}, f32[3,15,128]{2,1,0:T(8,128)S(1)}, u32[]{:S(2)}, u32[]{:S(2)}) collective-permute-start(f32[3,15,128]{2,1,0:T(8,128)S(1)} %get-tuple-element.19), channel_id=1, source_target_pairs={{0,1},{1,0},{2,3},{3,2},{4,5},{5,4},{6,7},{7,6},{8,9},{9,8},{10,11... | collective-permute-start | bytes 69128 | tf_op jit(solution)/shard_map/ppermute | solution.py:312
  18.0 4.4 %collective-permute-start.3 = (f32[2,15,512]{2,1,0:T(8,128)S(1)}, f32[2,15,512]{2,1,0:T(8,128)S(1)}, u32[]{:S(2)}, u32[]{:S(2)}) collective-permute-start(f32[2,15,512]{2,1,0:T(8,128)S(1)} %multiply_add_fusion.2), channel_id=1, source_target_pairs={{0,56},{8,48},{16,40},{24,32},{32,24},{40,16},{48,8},{56,0},{64,12... | collective-permute-start | bytes 184328 | tf_op jit(solution)/shard_map/ppermute | solution.py:312
  19.8 3.6 %collective-permute-start.9 = (f32[3,15,128]{2,1,0:T(8,128)S(1)}, f32[3,15,128]{2,1,0:T(8,128)S(1)}, u32[]{:S(2)}, u32[]{:S(2)}) collective-permute-start(f32[3,15,128]{2,1,0:T(8,128)S(1)} %pad_maximum_fusion.1), channel_id=1, source_target_pairs={{0,3},{1,2},{2,1},{3,0},{4,7},{5,6},{6,5},{7,4},{8,11},{9,10},{10,... | collective-permute-start | bytes 69128 | tf_op jit(solution)/shard_map/ppermute | solution.py:312
  23.5 9.0 %collective-permute-start.10 = (f32[3,15,128]{2,1,0:T(8,128)S(1)}, f32[3,15,128]{2,1,0:T(8,128)S(1)}, u32[]{:S(2)}, u32[]{:S(2)}) collective-permute-start(f32[3,15,128]{2,1,0:T(8,128)S(1)} %pad_maximum_fusion), channel_id=1, source_target_pairs={{0,7},{1,6},{2,5},{3,4},{4,3},{5,2},{6,1},{7,0},{8,15},{9,14},{10,... | collective-permute-start | bytes 69128 | tf_op jit(solution)/shard_map/ppermute | solution.py:312
  29.2 6.5 %collective-permute-start.6 = (f32[2,15,512]{2,1,0:T(8,128)S(1)}, f32[2,15,512]{2,1,0:T(8,128)S(1)}, u32[]{:S(2)}, u32[]{:S(2)}) collective-permute-start(f32[2,15,512]{2,1,0:T(8,128)S(1)} %multiply_add_fusion.1), channel_id=1, source_target_pairs={{0,192},{8,200},{16,208},{24,216},{32,224},{40,232},{48,240},{56,2... | collective-permute-start | bytes 184328 | tf_op jit(solution)/shard_map/ppermute | solution.py:312
  30.7 5.0 %collective-permute-start.5 = (f32[2,15,512]{2,1,0:T(8,128)S(1)}, f32[2,15,512]{2,1,0:T(8,128)S(1)}, u32[]{:S(2)}, u32[]{:S(2)}) collective-permute-start(f32[2,15,512]{2,1,0:T(8,128)S(1)} %multiply_add_fusion.1), channel_id=1, source_target_pairs={{0,128},{8,136},{16,144},{24,152},{32,160},{40,168},{48,176},{56,1... | collective-permute-start | bytes 184328 | tf_op jit(solution)/shard_map/ppermute | solution.py:312
  30.7 5.2 %collective-permute-start.4 = (f32[2,15,512]{2,1,0:T(8,128)S(1)}, f32[2,15,512]{2,1,0:T(8,128)S(1)}, u32[]{:S(2)}, u32[]{:S(2)}) collective-permute-start(f32[2,15,512]{2,1,0:T(8,128)S(1)} %multiply_add_fusion.1), channel_id=1, source_target_pairs={{0,64},{8,72},{16,80},{24,88},{32,96},{40,104},{48,112},{56,120},{... | collective-permute-start | bytes 184328 | tf_op jit(solution)/shard_map/ppermute | solution.py:312
  32.5 3.5 %copy-start.5 = (f32[128]{0:T(128)S(1)}, f32[128]{0:T(128)}, u32[]{:S(2)}) copy-start(f32[128]{0:T(128)} %param.10) | copy-start | bytes 1540
  32.6 3.5 %copy-start.6 = (f32[128,32]{1,0:T(8,128)S(1)}, f32[128,32]{1,0:T(8,128)}, u32[]{:S(2)}) copy-start(f32[128,32]{1,0:T(8,128)} %constant.17.clone.c_ref) | copy-start | bytes 49156
  32.6 3.5 %copy-start.7 = (f32[128,128]{1,0:T(8,128)S(1)}, f32[128,128]{1,0:T(8,128)}, u32[]{:S(2)}) copy-start(f32[128,128]{1,0:T(8,128)} %constant.16.clone.h_ref) | copy-start | bytes 196612

commit v4 on v3

--- a/solution.py
+++ b/solution.py
@@ -359,6 +359,9 @@
         if number == 1:
             reply = after(reply, total_x)
             replies_y[-1] = reply
+        if number == 2:
+            reply = after(reply, replies[0])
+            replies_y[-1] = reply
         at_y, total_y, outside_y = scan_round(rows[1], at_y, total_y, outside_y, [reply[:2]])
     outside_x = outside_x + rows[0, at_x : at_x + 2][:, None, None] * total_x
     outside_y = outside_y + rows[1, at_y : at_y + 2][:, None, None] * total_y

time: 38.5 us -> 40.7 us (1.057)
  starting transfers between devices: 25.2 us -> 27 us
  waiting for transfers between devices: 2.81 us -> 3.24 us
    ppermute x10, starting transfers between devices: 19.9 us -> 21.7 us  [swap(): lax.ppermute(block, axis, [(i, i ^ mask) for i in range(lax.axis_size(axi...]
    ppermute x10, waiting for transfers between devices: 2.73 us -> 3.16 us  [swap(): lax.ppermute(block, axis, [(i, i ^ mask) for i in range(lax.axis_size(axi...]
  transfers between devices with their start and end apart: 11 -> 11, of which waited for: 5 -> 4; matrix products, arithmetic and copies ran while one was open for 1% -> 1% of each run, Pallas kernels for 11% -> 3%
where the time goes in v4:
time: 40.7 us; the launch traced here: 40.6 us
  starting transfers between devices  27 us (66%)
  Pallas kernels  8.8 us (22%)
  waiting for transfers between devices  3.24 us (8%)
  between operations  0.81 us (2%)
  other arithmetic  0.54 us (1%)
    ppermute x10, starting transfers between devices, swap(): lax.ppermute(block, axis, [(i, i ^ mask) for i in range(lax.axis_size(axi...  21.7 us
    ppermute x1, starting transfers between devices, swap_odd(): lax.ppermute(block, axis, [(i, (i + (1 if i % 2 else -1)) % count) for i...  5.33 us
    ppermute x10, waiting for transfers between devices, swap(): lax.ppermute(block, axis, [(i, i ^ mask) for i in range(lax.axis_size(axi...  3.16 us
    pallas_call x1, Pallas kernels, second(): pl.pallas_call(second_kernel, in_specs=[pl.BlockSpec(memory_space=pltpu.V...  3.06 us
    pallas_call x1, Pallas kernels, first(): pl.pallas_call(first_kernel, in_specs=[pl.BlockSpec(memory_space=pltpu.VM...  2.34 us
    pallas_call x1, Pallas kernels, first_moments(): pl.pallas_call(first_moments_kernel, in_specs=[pl.BlockSpec(memory_space=...  2.29 us
    pallas_call x1, Pallas kernels, second_moments(): pl.pallas_call(second_moments_kernel, in_specs=[pl.BlockSpec(memory_space...  1.12 us
  transfers between devices with their start and end apart: 11, of which 4 were waited for; matrix products, arithmetic and copies ran while one was open for 1% of the time, Pallas kernels for 3%

profile of v4, /device:TPU:1, one launch (start us, length us, event | category | flops | bytes accessed | tf_op | source)
XLA Modules:
  0.0 40.6 jit_solution(13170044131384996813)
XLA Ops:
  0.6 0.0 copy-start.3
  0.6 0.0 copy-start.2
  0.7 0.0 copy-start.6
  0.7 0.0 copy-start.7
  0.7 2.3 %moments_first.1 = (f32[15,128,512]{2,1,0:T(8,128)S(1)}, f32[3,15,512]{2,1,0:T(8,128)S(1)}, f32[2,15,512]{2,1,0:T(8,128)S(1)}, f32[15,512]{1,0:T(8,128)S(1)}) custom-call(f32[15,128,512]{2,1,0:T(8,128)} %bitcast.64), custom_call_target="tpu_custom_call" | custom-call | flops 8000000 | bytes 8000000 | tf_op jit(solution)/shard_map/moments_first/pallas_call | solution.py:101
  3.0 5.3 %collective-permute-start.2 = (f32[2,15,512]{2,1,0:T(8,128)S(1)}, f32[2,15,512]{2,1,0:T(8,128)S(1)}, u32[]{:S(2)}, u32[]{:S(2)}) collective-permute-start(f32[2,15,512]{2,1,0:T(8,128)S(1)} %get-tuple-element.18), channel_id=1, source_target_pairs={{0,24},{8,16},{16,8},{24,0},{32,56},{40,48},{48,40},{56,32},{64,88... | collective-permute-start | bytes 184328 | tf_op jit(solution)/shard_map/ppermute | solution.py:312
  8.2 0.0 collective-permute-start.1
  8.2 5.3 %collective-permute-start.7 = (f32[15,512]{1,0:T(8,128)S(1)}, f32[15,512]{1,0:T(8,128)S(1)}, u32[]{:S(2)}, u32[]{:S(2)}) collective-permute-start(f32[15,512]{1,0:T(8,128)S(1)} %get-tuple-element.15.after_ref), channel_id=1, source_target_pairs={{0,248},{8,16},{16,8},{24,32},{32,24},{40,48},{48,40},{56,64},{64,... | collective-permute-start | bytes 92168 | tf_op jit(solution)/shard_map/ppermute | solution.py:317
  13.6 1.1 %moments_second.1 = (f32[3,15,128]{2,1,0:T(8,128)S(1)}, f32[5,15,128]{2,1,0:T(8,128)S(1)}, f32[2,128]{1,0:T(2,128)S(1)}) custom-call(f32[15,128,512]{2,1,0:T(8,128)S(1)} %get-tuple-element.14.u_ref, f32[15,512]{1,0:T(8,128)S(1)} %get-tuple-element.15.after_ref, f32[32,128]{1,0:T(8,128)S(1)} %copy-done.2, f32[8,128]{1,0:T(8,128)S(1)} %copy-done.3), custom_call_target="tpu_custom_call" | custom-call | flops 8000000 | bytes 8000000 | tf_op jit(solution)/shard_map/moments_second/pallas_call | solution.py:147
  14.7 0.1 slice_bitcast_fusion.9
  14.8 0.1 collective-permute-done.7.far_ref
  14.9 2.1 %collective-permute-start.8 = (f32[3,15,128]{2,1,0:T(8,128)S(1)}, f32[3,15,128]{2,1,0:T(8,128)S(1)}, u32[]{:S(2)}, u32[]{:S(2)}) collective-permute-start(f32[3,15,128]{2,1,0:T(8,128)S(1)} %get-tuple-element.20), channel_id=1, source_target_pairs={{0,1},{1,0},{2,3},{3,2},{4,5},{5,4},{6,7},{7,6},{8,9},{9,8},{10,11... | collective-permute-start | bytes 69128 | tf_op jit(solution)/shard_map/ppermute | solution.py:312
  17.0 0.1 slice_bitcast_fusion.27
  17.1 0.8 %collective-permute-done.8.near_ref = f32[3,15,128]{2,1,0:T(8,128)S(1)} collective-permute-done((f32[3,15,128]{2,1,0:T(8,128)S(1)}, f32[3,15,128]{2,1,0:T(8,128)S(1)}, u32[]{:S(2)}, u32[]{:S(2)}) %collective-permute-start.8) | collective-permute-done | bytes 23072 | tf_op jit(solution)/shard_map/ppermute | solution.py:312
  17.8 0.1 multiply_add_fusion.5
  17.9 0.1 multiply_add_fusion.2
  18.0 1.7 %collective-permute-start.3 = (f32[2,15,512]{2,1,0:T(8,128)S(1)}, f32[2,15,512]{2,1,0:T(8,128)S(1)}, u32[]{:S(2)}, u32[]{:S(2)}) collective-permute-start(f32[2,15,512]{2,1,0:T(8,128)S(1)} %multiply_add_fusion.2), channel_id=1, source_target_pairs={{0,56},{8,48},{16,40},{24,32},{32,24},{40,16},{48,8},{56,0},{64,12... | collective-permute-start | bytes 184328 | tf_op jit(solution)/shard_map/ppermute | solution.py:312
  19.8 1.8 %collective-permute-start.9 = (f32[3,15,128]{2,1,0:T(8,128)S(1)}, f32[3,15,128]{2,1,0:T(8,128)S(1)}, u32[]{:S(2)}, u32[]{:S(2)}) collective-permute-start(f32[3,15,128]{2,1,0:T(8,128)S(1)} %pad_maximum_fusion.1), channel_id=1, source_target_pairs={{0,3},{1,2},{2,1},{3,0},{4,7},{5,6},{6,5},{7,4},{8,11},{9,10},{10,... | collective-permute-start | bytes 69128 | tf_op jit(solution)/shard_map/ppermute | solution.py:312
  21.6 0.9 %collective-permute-done.3 = f32[2,15,512]{2,1,0:T(8,128)S(1)} collective-permute-done((f32[2,15,512]{2,1,0:T(8,128)S(1)}, f32[2,15,512]{2,1,0:T(8,128)S(1)}, u32[]{:S(2)}, u32[]{:S(2)}) %collective-permute-start.3) | collective-permute-done | bytes 61472 | tf_op jit(solution)/shard_map/ppermute | solution.py:312
  22.4 0.1 multiply_add_fusion.1
  22.5 5.0 %collective-permute-start.6 = (f32[2,15,512]{2,1,0:T(8,128)S(1)}, f32[2,15,512]{2,1,0:T(8,128)S(1)}, u32[]{:S(2)}, u32[]{:S(2)}) collective-permute-start(f32[2,15,512]{2,1,0:T(8,128)S(1)} %multiply_add_fusion.1), channel_id=1, source_target_pairs={{0,192},{8,200},{16,208},{24,216},{32,224},{40,232},{48,240},{56,2... | collective-permute-start | bytes 184328 | tf_op jit(solution)/shard_map/ppermute | solution.py:312
  27.6 0.7 %collective-permute-start.4 = (f32[2,15,512]{2,1,0:T(8,128)S(1)}, f32[2,15,512]{2,1,0:T(8,128)S(1)}, u32[]{:S(2)}, u32[]{:S(2)}) collective-permute-start(f32[2,15,512]{2,1,0:T(8,128)S(1)} %multiply_add_fusion.1), channel_id=1, source_target_pairs={{0,64},{8,72},{16,80},{24,88},{32,96},{40,104},{48,112},{56,120},{... | collective-permute-start | bytes 184328 | tf_op jit(solution)/shard_map/ppermute | solution.py:312
  28.2 0.1 multiply_add_fusion.4
  28.3 5.0 %collective-permute-start.10 = (f32[3,15,128]{2,1,0:T(8,128)S(1)}, f32[3,15,128]{2,1,0:T(8,128)S(1)}, u32[]{:S(2)}, u32[]{:S(2)}) collective-permute-start(f32[3,15,128]{2,1,0:T(8,128)S(1)} %pad_maximum_fusion), channel_id=1, source_target_pairs={{0,7},{1,6},{2,5},{3,4},{4,3},{5,2},{6,1},{7,0},{8,15},{9,14},{10,... | collective-permute-start | bytes 69128 | tf_op jit(solution)/shard_map/ppermute | solution.py:312
  33.4 1.5 %collective-permute-done.10.seven_ref = f32[3,15,128]{2,1,0:T(8,128)S(1)} collective-permute-done((f32[3,15,128]{2,1,0:T(8,128)S(1)}, f32[3,15,128]{2,1,0:T(8,128)S(1)}, u32[]{:S(2)}, u32[]{:S(2)}) %collective-permute-start.10) | collective-permute-done | bytes 23072 | tf_op jit(solution)/shard_map/ppermute | solution.py:312
  34.9 0.1 multiply_add_fusion.v_ref
  35.0 0.0 copy-start
  35.1 0.0 copy-start.1
  35.1 0.0 copy-start.4
  35.1 2.3 %slope_first.1 = f32[15,128,512]{2,1,0:T(8,128)} custom-call(f32[15,128,512]{2,1,0:T(8,128)S(1)} %get-tuple-element.14.u_ref, f32[2,15,512]{2,1,0:T(8,128)S(1)} %multiply_add_fusion.v_ref, f32[15,512]{1,0:T(8,128)S(1)} %collective-permute-done.7.far_ref, f32[3,15,512]{2,1,0:T(8,128)S(1)} %collective-permute-done.near_ref, f32[1,128]{1,0:T(1,128)S(1)} %bitcast.62, ...), custom_call_target="tpu_custom_call" | custom-call | flops 3000000000 | bytes 8000000 | tf_op jit(solution)/shard_map/slope_first/pallas_call | solution.py:201
  37.4 0.1 multiply_add_fusion.3.outside_ref
  37.6 3.1 %slope_second.1 = f32[15,128,512]{2,1,0:T(8,128)} custom-call(f32[15,128,512]{2,1,0:T(8,128)S(1)} %get-tuple-element.14.u_ref, f32[2,15,128]{2,1,0:T(8,128)S(1)} %multiply_add_fusion.3.outside_ref, f32[5,15,128]{2,1,0:T(8,128)S(1)} %get-tuple-element.21.own_ref, f32[3,15,128]{2,1,0:T(8,128)S(1)} %collective-permute-done.8.near_ref, ...), custom_call_target="tpu_custom_call" | custom-call | flops 300000000 | bytes 8000000 | tf_op jit(solution)/shard_map/slope_second/pallas_call | solution.py:275
  (21 shorter events, 0.1 us)
Async XLA Ops:
  0.6 13.0 %copy-start.3 = (f32[8,128]{1,0:T(8,128)S(1)}, f32[8,128]{1,0:T(8,128)}, u32[]{:S(2)}) copy-start(f32[8,128]{1,0:T(8,128)} %constant.13.clone.wy_ref) | copy-start | bytes 12292
  0.6 13.0 %copy-start.2 = (f32[32,128]{1,0:T(8,128)S(1)}, f32[32,128]{1,0:T(8,128)}, u32[]{:S(2)}) copy-start(f32[32,128]{1,0:T(8,128)} %constant.12.clone.wx_ref) | copy-start | bytes 49156
  0.7 34.4 %copy-start.5 = (f32[128]{0:T(128)S(1)}, f32[128]{0:T(128)}, u32[]{:S(2)}) copy-start(f32[128]{0:T(128)} %param.10) | copy-start | bytes 1540
  0.7 34.4 %copy-start.6 = (f32[128,32]{1,0:T(8,128)S(1)}, f32[128,32]{1,0:T(8,128)}, u32[]{:S(2)}) copy-start(f32[128,32]{1,0:T(8,128)} %constant.17.clone.c_ref) | copy-start | bytes 49156
  0.7 34.4 %copy-start.7 = (f32[128,128]{1,0:T(8,128)S(1)}, f32[128,128]{1,0:T(8,128)}, u32[]{:S(2)}) copy-start(f32[128,128]{1,0:T(8,128)} %constant.16.clone.h_ref) | copy-start | bytes 196612
  3.0 14.9 %collective-permute-start.2 = (f32[2,15,512]{2,1,0:T(8,128)S(1)}, f32[2,15,512]{2,1,0:T(8,128)S(1)}, u32[]{:S(2)}, u32[]{:S(2)}) collective-permute-start(f32[2,15,512]{2,1,0:T(8,128)S(1)} %get-tuple-element.18), channel_id=1, source_target_pairs={{0,24},{8,16},{16,8},{24,0},{32,56},{40,48},{48,40},{56,32},{64,88... | collective-permute-start | bytes 184328 | tf_op jit(solution)/shard_map/ppermute | solution.py:312
  8.2 9.7 %collective-permute-start.1 = (f32[2,15,512]{2,1,0:T(8,128)S(1)}, f32[2,15,512]{2,1,0:T(8,128)S(1)}, u32[]{:S(2)}, u32[]{:S(2)}) collective-permute-start(f32[2,15,512]{2,1,0:T(8,128)S(1)} %get-tuple-element.18), channel_id=1, source_target_pairs={{0,16},{8,24},{16,0},{24,8},{32,48},{40,56},{48,32},{56,40},{64,80... | collective-permute-start | bytes 184328 | tf_op jit(solution)/shard_map/ppermute | solution.py:312
  8.2 6.6 %collective-permute-start.7 = (f32[15,512]{1,0:T(8,128)S(1)}, f32[15,512]{1,0:T(8,128)S(1)}, u32[]{:S(2)}, u32[]{:S(2)}) collective-permute-start(f32[15,512]{1,0:T(8,128)S(1)} %get-tuple-element.15.after_ref), channel_id=1, source_target_pairs={{0,248},{8,16},{16,8},{24,32},{32,24},{40,48},{48,40},{56,64},{64,... | collective-permute-start | bytes 92168 | tf_op jit(solution)/shard_map/ppermute | solution.py:317
  13.6 4.3 %collective-permute-start = (f32[3,15,512]{2,1,0:T(8,128)S(1)}, f32[3,15,512]{2,1,0:T(8,128)S(1)}, u32[]{:S(2)}, u32[]{:S(2)}) collective-permute-start(f32[3,15,512]{2,1,0:T(8,128)S(1)} %get-tuple-element.17), channel_id=1, source_target_pairs={{0,8},{8,0},{16,24},{24,16},{32,40},{40,32},{48,56},{56,48},{64,72... | collective-permute-start | bytes 276488 | tf_op jit(solution)/shard_map/ppermute | solution.py:312
  14.9 3.0 %collective-permute-start.8 = (f32[3,15,128]{2,1,0:T(8,128)S(1)}, f32[3,15,128]{2,1,0:T(8,128)S(1)}, u32[]{:S(2)}, u32[]{:S(2)}) collective-permute-start(f32[3,15,128]{2,1,0:T(8,128)S(1)} %get-tuple-element.20), channel_id=1, source_target_pairs={{0,1},{1,0},{2,3},{3,2},{4,5},{5,4},{6,7},{7,6},{8,9},{9,8},{10,11... | collective-permute-start | bytes 69128 | tf_op jit(solution)/shard_map/ppermute | solution.py:312
  18.0 4.4 %collective-permute-start.3 = (f32[2,15,512]{2,1,0:T(8,128)S(1)}, f32[2,15,512]{2,1,0:T(8,128)S(1)}, u32[]{:S(2)}, u32[]{:S(2)}) collective-permute-start(f32[2,15,512]{2,1,0:T(8,128)S(1)} %multiply_add_fusion.2), channel_id=1, source_target_pairs={{0,56},{8,48},{16,40},{24,32},{32,24},{40,16},{48,8},{56,0},{64,12... | collective-permute-start | bytes 184328 | tf_op jit(solution)/shard_map/ppermute | solution.py:312
  19.8 8.5 %collective-permute-start.9 = (f32[3,15,128]{2,1,0:T(8,128)S(1)}, f32[3,15,128]{2,1,0:T(8,128)S(1)}, u32[]{:S(2)}, u32[]{:S(2)}) collective-permute-start(f32[3,15,128]{2,1,0:T(8,128)S(1)} %pad_maximum_fusion.1), channel_id=1, source_target_pairs={{0,3},{1,2},{2,1},{3,0},{4,7},{5,6},{6,5},{7,4},{8,11},{9,10},{10,... | collective-permute-start | bytes 69128 | tf_op jit(solution)/shard_map/ppermute | solution.py:312
  22.5 12.4 %collective-permute-start.6 = (f32[2,15,512]{2,1,0:T(8,128)S(1)}, f32[2,15,512]{2,1,0:T(8,128)S(1)}, u32[]{:S(2)}, u32[]{:S(2)}) collective-permute-start(f32[2,15,512]{2,1,0:T(8,128)S(1)} %multiply_add_fusion.1), channel_id=1, source_target_pairs={{0,192},{8,200},{16,208},{24,216},{32,224},{40,232},{48,240},{56,2... | collective-permute-start | bytes 184328 | tf_op jit(solution)/shard_map/ppermute | solution.py:312
  27.6 7.3 %collective-permute-start.5 = (f32[2,15,512]{2,1,0:T(8,128)S(1)}, f32[2,15,512]{2,1,0:T(8,128)S(1)}, u32[]{:S(2)}, u32[]{:S(2)}) collective-permute-start(f32[2,15,512]{2,1,0:T(8,128)S(1)} %multiply_add_fusion.1), channel_id=1, source_target_pairs={{0,128},{8,136},{16,144},{24,152},{32,160},{40,168},{48,176},{56,1... | collective-permute-start | bytes 184328 | tf_op jit(solution)/shard_map/ppermute | solution.py:312
  27.6 7.3 %collective-permute-start.4 = (f32[2,15,512]{2,1,0:T(8,128)S(1)}, f32[2,15,512]{2,1,0:T(8,128)S(1)}, u32[]{:S(2)}, u32[]{:S(2)}) collective-permute-start(f32[2,15,512]{2,1,0:T(8,128)S(1)} %multiply_add_fusion.1), channel_id=1, source_target_pairs={{0,64},{8,72},{16,80},{24,88},{32,96},{40,104},{48,112},{56,120},{... | collective-permute-start | bytes 184328 | tf_op jit(solution)/shard_map/ppermute | solution.py:312
  28.3 6.6 %collective-permute-start.10 = (f32[3,15,128]{2,1,0:T(8,128)S(1)}, f32[3,15,128]{2,1,0:T(8,128)S(1)}, u32[]{:S(2)}, u32[]{:S(2)}) collective-permute-start(f32[3,15,128]{2,1,0:T(8,128)S(1)} %pad_maximum_fusion), channel_id=1, source_target_pairs={{0,7},{1,6},{2,5},{3,4},{4,3},{5,2},{6,1},{7,0},{8,15},{9,14},{10,... | collective-permute-start | bytes 69128 | tf_op jit(solution)/shard_map/ppermute | solution.py:312
  35.0 2.5 %copy-start = (bf16[2,256,256]{2,1,0:T(8,128)(2,1)S(1)}, bf16[2,256,256]{2,1,0:T(8,128)(2,1)}, u32[]{:S(2)}) copy-start(bf16[2,256,256]{2,1,0:T(8,128)(2,1)} %constant.14.clone.h_ref) | copy-start | bytes 786436
  35.1 2.5 %copy-start.1 = (bf16[32,512]{1,0:T(8,128)(2,1)S(1)}, bf16[32,512]{1,0:T(8,128)(2,1)}, u32[]{:S(2)}) copy-start(bf16[32,512]{1,0:T(8,128)(2,1)} %constant.15.clone.c_ref) | copy-start | bytes 98308
  35.1 2.5 %copy-start.4 = (f32[512]{0:T(512)S(1)}, f32[512]{0:T(512)}, u32[]{:S(2)}) copy-start(f32[512]{0:T(512)} %param.11) | copy-start | bytes 6148
